TPU v7x, 128 devices: a whole 4x4x4 slice. The times are simulated.
128 devices in a mesh: req: 8 (over x, core), exp: 16 (over y, z).
Axes of the slice: x: 4, y: 4, z: 4, core: 2. Of those that a mesh axis runs over, the one named last changes fastest.
Arguments:
- tokens: bfloat16 [8320, 2048], P('req'), may hold values from -6 to 6
- attn_gain: bfloat16 [2048], replicated, may hold values from 0.099609375 to 1.8984375
- wq_nope: bfloat16 [2048, 2048], P(None, 'exp'), may hold values from -0.125 to 0.125
- wq_rope: bfloat16 [2048, 1024], P(None, 'exp'), may hold values from -0.125 to 0.125
- w_latent: bfloat16 [2048, 512], replicated, may hold values from -0.125 to 0.125
- w_krope: bfloat16 [2048, 64], replicated, may hold values from -0.125 to 0.125
- latent_gain: bfloat16 [512], replicated, may hold values from 0.099609375 to 1.8984375
- w_uk: bfloat16 [512, 2048], P(None, 'exp'), may hold values from -0.25 to 0.25
- w_uv: bfloat16 [512, 2048], P(None, 'exp'), may hold values from -0.25 to 0.25
- w_out: bfloat16 [2048, 2048], P('exp'), may hold values from -0.125 to 0.125
- moe_gain: bfloat16 [2048], replicated, may hold values from 0.099609375 to 1.8984375
- w_router: bfloat16 [2048, 64], replicated, may hold values from -0.125 to 0.125
- w_gate: bfloat16 [128, 2048, 704], P(('req', 'exp')), may hold values from -0.125 to 0.125
- w_up: bfloat16 [128, 2048, 704], P(('req', 'exp')), may hold values from -0.125 to 0.125
- w_down: bfloat16 [128, 704, 2048], P(('req', 'exp')), may hold values from -0.15625 to 0.15625
- routes: int32 [8320, 6], P(('req', 'exp')), may hold values from 0 to 63, all different within a row; in each aligned block of 65 rows (0 to 64, 65 to 129, ...) at most 10 rows name the same one
- cache_latent: bfloat16 [128, 16, 32, 512], P('req', 'exp'), may hold values from -300 to 300
- cache_rope: bfloat16 [128, 16, 2048], P('req', 'exp'), may hold values from -6 to 6
- mig_dest: int32 [128], P('req'), may hold values from 0 to 7, as said below
- page_table: int32 [128, 16], P('req'), may hold values from 0 to 15, each once within a row
- cache_len: int32 [128], P('req'), may hold values from 1 to 512
- span_slot: int32 [8], P('req'), may hold values from 0 to 15
Outputs:
- mixed: bfloat16 [8320, 2048], P(('req', 'exp'))
Inputs may be any that keep to these rules, and one draw needn't show every extreme that they name: `routes`: among the rows of one device, no expert is named by more than 10 rows, a bound that some block reaches. `mig_dest`: among the 16 slots of each group, exactly 2 go to each group, itself included.
All inputs are finite; a program needn't handle non-finite values.
Results may differ from a plain program's by a relative error of at most 0.019.
The roundings to bfloat16 on the way count: a program that leaves them out, or rounds other values in their place, can miss the bound.
Values may be sent and summed in bfloat16 or wider, within the bound.
No kernel may reach another device: no remote copies, remote signals or barrier semaphores. Data moves between devices by JAX's collectives and lax.ppermute only.
A program may use at most 128 MiB of HBM per device.

v0:
```python
import math

import jax
import jax.numpy as jnp
from jax import lax
from jax.sharding import PartitionSpec as P

DN = 128
DR = 64
TOP = 6
SPAN = 1024


theta_base = 50000.0
route_scale = 2.446
norm_eps = 1e-06


def rms_scale(values, gain_values):
    widened = values.astype(jnp.float32)
    mean_square = jnp.mean(widened * widened, axis=-1, keepdims=True)
    return widened * lax.rsqrt(mean_square + norm_eps) * gain_values.astype(jnp.float32)


def rope_angles(positions, rope_width):
    exponent = jnp.arange(rope_width // 2, dtype=jnp.float32) * (2.0 / rope_width)
    frequency = jnp.exp(-exponent * math.log(theta_base))
    return positions.astype(jnp.float32)[:, None] * frequency[None, :]


def rotate(values, angles):
    half_width = values.shape[-1] // 2
    cosine = jnp.cos(angles)
    sine_part = jnp.sin(angles)
    first_half = values[..., :half_width]
    second_half = values[..., half_width:]
    return jnp.concatenate(
        [
            first_half * cosine - second_half * sine_part,
            second_half * cosine + first_half * sine_part,
        ],
        axis=-1,
    )


def group_positions(lengths, span_slots, span_width):
    starts = jnp.take(lengths, span_slots)
    span_positions = starts[:, None] + jnp.arange(span_width, dtype=jnp.int32)[None, :]
    return jnp.concatenate([span_positions.reshape(-1), lengths])


def dot_transposed(left_side, right_side):
    return lax.dot_general(
        left_side, right_side, (((1,), (1,)), ((), ())), preferred_element_type=jnp.float32
    )


def soft_weights(scores, visible):
    masked = jnp.where(visible, scores, -jnp.inf)
    row_top = jnp.max(masked, axis=-1, keepdims=True)
    raised = jnp.where(visible, jnp.exp(masked - row_top), 0.0)
    return (raised / jnp.sum(raised, axis=-1, keepdims=True)).astype(jnp.bfloat16)


def attend_head(
    query_latent,
    query_rope,
    new_latent,
    new_rope,
    cache_keys,
    cache_rope_keys,
    lengths,
    span_slots,
    span_width,
    scale_factor,
):
    cache_size = cache_keys.shape[1]
    key_index = jnp.arange(cache_size + span_width, dtype=jnp.int32)
    row_index = jnp.arange(span_width, dtype=jnp.int32)
    results = []
    request = span_slots[0]
    keys_latent = jnp.concatenate([cache_keys[request], new_latent[0:span_width]], axis=0)
    keys_rope = jnp.concatenate([cache_rope_keys[request], new_rope[0:span_width]], axis=0)
    scores = (
        dot_transposed(query_latent[0:span_width], keys_latent)
        + dot_transposed(query_rope[0:span_width], keys_rope)
    ) * scale_factor
    visible = jnp.where(
        key_index[None, :] < cache_size,
        key_index[None, :] < lengths[request],
        key_index[None, :] - cache_size <= row_index[:, None],
    )
    weights = soft_weights(scores, visible)
    results.append(
        jnp.dot(weights, keys_latent, preferred_element_type=jnp.float32).astype(jnp.bfloat16)
    )
    dec_start = span_slots.shape[0] * span_width
    dec_latent = query_latent[dec_start:]
    dec_rope = query_rope[dec_start:]
    own_latent = new_latent[dec_start:]
    own_rope = new_rope[dec_start:]
    cache_scores = (
        jnp.einsum("jr,jpr->jp", dec_latent, cache_keys, preferred_element_type=jnp.float32)
        + jnp.einsum("je,jpe->jp", dec_rope, cache_rope_keys, preferred_element_type=jnp.float32)
    ) * scale_factor
    self_scores = (
        jnp.sum(dec_latent.astype(jnp.float32) * own_latent.astype(jnp.float32), axis=1)
        + jnp.sum(dec_rope.astype(jnp.float32) * own_rope.astype(jnp.float32), axis=1)
    ) * scale_factor
    seen = jnp.arange(cache_size, dtype=jnp.int32)[None, :] < lengths[:, None]
    masked = jnp.where(seen, cache_scores, -jnp.inf)
    row_top = jnp.maximum(jnp.max(masked, axis=1), self_scores)
    cache_raised = jnp.where(seen, jnp.exp(masked - row_top[:, None]), 0.0)
    self_raised = jnp.exp(self_scores - row_top)
    totals = jnp.sum(cache_raised, axis=1) + self_raised
    cache_weights = (cache_raised / totals[:, None]).astype(jnp.bfloat16)
    self_weights = (self_raised / totals).astype(jnp.bfloat16)
    dec_out = jnp.einsum(
        "jp,jpr->jr", cache_weights, cache_keys, preferred_element_type=jnp.float32
    ) + self_weights.astype(jnp.float32)[:, None] * own_latent.astype(jnp.float32)
    results.append(dec_out.astype(jnp.bfloat16))
    return jnp.concatenate(results, axis=0)


def one_half(inputs, gate_part, up_part, down_part):
    hidden = (
        jax.nn.silu(jnp.dot(inputs, gate_part, preferred_element_type=jnp.float32))
        * jnp.dot(inputs, up_part, preferred_element_type=jnp.float32)
    ).astype(jnp.bfloat16)
    return jnp.dot(hidden, down_part, preferred_element_type=jnp.float32).astype(jnp.bfloat16)


def expert_halves(received, w_gate, w_up, w_down):
    sources, halves, slot_count, model_width = received.shape
    inputs = received[:, 0].reshape(sources * slot_count, model_width)
    output = one_half(inputs, w_gate[0], w_up[0], w_down[0])
    results = [output.reshape(sources, slot_count, model_width)]
    return jnp.stack(results, axis=1)


def shards(
    tokens,
    attn_gain,
    wq_nope,
    wq_rope,
    w_latent,
    w_krope,
    latent_gain,
    w_uk,
    w_uv,
    w_out,
    moe_gain,
    w_router,
    w_gate,
    w_up,
    w_down,
    routes,
    cache_latent,
    cache_rope,
    mig_dest,
    page_table,
    cache_len,
    span_slot,
):
    req_count = lax.axis_size("req")
    exp_count = lax.axis_size("exp")
    device_count = req_count * exp_count
    req_group = mig_dest.shape[0]
    move_count = req_group // req_count
    rows_group = tokens.shape[0]
    rows_device = rows_group // exp_count
    model_width = tokens.shape[1]
    heads_device = wq_nope.shape[1] // DN
    scale_factor = 1.0 / math.sqrt(DN + DR)
    slot_ids = jnp.arange(req_group, dtype=jnp.int32)
    earlier = (mig_dest[None, :] == mig_dest[:, None]) & (slot_ids[None, :] < slot_ids[:, None])
    placed = mig_dest * move_count + jnp.sum(earlier.astype(jnp.int32), axis=1)
    source_slot = jnp.argmax((placed[None, :] == slot_ids[:, None]).astype(jnp.int32), axis=1)
    outgoing_latent = cache_latent[source_slot].reshape(
        (req_count, move_count) + cache_latent.shape[1:]
    )
    outgoing_rope = cache_rope[source_slot].reshape((req_count, move_count) + cache_rope.shape[1:])
    arrived = (
        lax.all_to_all(outgoing_latent, "req", split_axis=0, concat_axis=0, tiled=True),
        lax.all_to_all(outgoing_rope, "req", split_axis=0, concat_axis=0, tiled=True),
    )
    local_latent = arrived[0].reshape(cache_latent.shape)
    local_rope = arrived[1].reshape(cache_rope.shape)
    whole_latent, whole_rope = (
        lax.all_gather(local_latent, "exp", axis=1, tiled=True),
        lax.all_gather(local_rope, "exp", axis=1, tiled=True),
    )
    cache_keys = jnp.take_along_axis(whole_latent, page_table[:, :, None, None], axis=1).reshape(
        req_group, -1, whole_latent.shape[-1]
    )
    cache_rope_keys = jnp.take_along_axis(whole_rope, page_table[:, :, None], axis=1).reshape(
        req_group, -1, DR
    )
    normed = rms_scale(tokens, attn_gain).astype(jnp.bfloat16)
    angles = rope_angles(group_positions(cache_len, span_slot, SPAN), DR)
    query_nope = jnp.dot(normed, wq_nope, preferred_element_type=jnp.float32).astype(jnp.bfloat16)
    query_rope = rotate(
        jnp.dot(normed, wq_rope, preferred_element_type=jnp.float32).reshape(
            rows_group, heads_device, DR
        ),
        angles[:, None, :],
    ).astype(jnp.bfloat16)
    row_offset = lax.axis_index("exp") * rows_device
    own_normed = lax.dynamic_slice_in_dim(normed, row_offset, rows_device, 0)
    own_angles = lax.dynamic_slice_in_dim(angles, row_offset, rows_device, 0)
    own_latent = rms_scale(
        jnp.dot(own_normed, w_latent, preferred_element_type=jnp.float32), latent_gain
    ).astype(jnp.bfloat16)
    own_rope = rotate(
        jnp.dot(own_normed, w_krope, preferred_element_type=jnp.float32), own_angles
    ).astype(jnp.bfloat16)
    new_latent, new_rope = (
        lax.all_gather(own_latent, "exp", axis=0, tiled=True),
        lax.all_gather(own_rope, "exp", axis=0, tiled=True),
    )
    query_latent = dot_transposed(query_nope, w_uk).astype(jnp.bfloat16)
    attended = attend_head(
        query_latent,
        query_rope[:, 0],
        new_latent,
        new_rope,
        cache_keys,
        cache_rope_keys,
        cache_len,
        span_slot,
        SPAN,
        scale_factor,
    )
    head_outs = jnp.dot(attended, w_uv, preferred_element_type=jnp.float32).astype(jnp.bfloat16)
    attn_rows = lax.psum_scatter(
        jnp.dot(head_outs, w_out, preferred_element_type=jnp.float32).astype(jnp.bfloat16),
        "exp",
        scatter_dimension=0,
        tiled=True,
    ).astype(jnp.float32)
    own_tokens = lax.dynamic_slice_in_dim(tokens, row_offset, rows_device, 0)
    resid = (own_tokens.astype(jnp.float32) + attn_rows).astype(jnp.bfloat16)
    moe_in = rms_scale(resid, moe_gain).astype(jnp.bfloat16)
    picked = jnp.take_along_axis(
        jax.nn.sigmoid(jnp.dot(moe_in, w_router, preferred_element_type=jnp.float32)),
        routes,
        axis=1,
    )
    gate_w = route_scale * picked / jnp.sum(picked, axis=1, keepdims=True)
    expert_count = w_router.shape[1]
    capacity = 2 * ((rows_device * TOP // expert_count + 5) // 2)
    flat_routes = routes.reshape(-1)
    onehot = (flat_routes[:, None] == jnp.arange(expert_count, dtype=jnp.int32)[None, :]).astype(
        jnp.int32
    )
    slot_rank = jnp.sum((jnp.cumsum(onehot, axis=0) - 1) * onehot, axis=1)
    slot_of = flat_routes * capacity + slot_rank
    slot_index = jnp.arange(expert_count * capacity, dtype=jnp.int32)
    dispatch_rows = jnp.any(
        (slot_of[None, :] == slot_index[:, None]).reshape(
            expert_count * capacity, rows_device, TOP
        ),
        axis=2,
    ).astype(jnp.bfloat16)
    packed = jnp.dot(dispatch_rows, moe_in, preferred_element_type=jnp.float32).astype(jnp.bfloat16)
    halves_device = w_gate.shape[0]
    doubled = jnp.broadcast_to(
        packed.reshape(expert_count, 1, capacity, model_width),
        (expert_count, 2, capacity, model_width),
    ).reshape(device_count, halves_device, capacity, model_width)
    computed = expert_halves(
        lax.all_to_all(doubled, ("req", "exp"), split_axis=0, concat_axis=0, tiled=True),
        w_gate,
        w_up,
        w_down,
    )
    returned = lax.all_to_all(computed, ("req", "exp"), split_axis=0, concat_axis=0, tiled=True)
    paired = returned.reshape(expert_count, 2, capacity, model_width)
    expert_out = (
        (paired[:, 0].astype(jnp.float32) + paired[:, 1].astype(jnp.float32))
        .astype(jnp.bfloat16)
        .reshape(expert_count * capacity, model_width)
    )
    gathered = expert_out[slot_of].astype(jnp.float32).reshape(rows_device, TOP, model_width)
    moe_out = jnp.sum(gate_w[:, :, None] * gathered, axis=1)
    return (resid.astype(jnp.float32) + moe_out).astype(jnp.bfloat16)


def solution(mesh):
    in_specs = (
        P("req", None),
        P(),
        P(None, "exp"),
        P(None, "exp"),
        P(),
        P(),
        P(),
        P(None, "exp"),
        P(None, "exp"),
        P("exp", None),
        P(),
        P(),
        P(("req", "exp"), None, None),
        P(("req", "exp"), None, None),
        P(("req", "exp"), None, None),
        P(("req", "exp"), None),
        P("req", "exp", None, None),
        P("req", "exp", None),
        P("req"),
        P("req", None),
        P("req"),
        P("req"),
    )
    out_specs = P(("req", "exp"), None)
    return jax.shard_map(shards, mesh=mesh, in_specs=in_specs, out_specs=out_specs, check_vma=False)
```

profile of v0, /device:TPU:32, one launch (start us, length us, event | category | flops | bytes accessed | tf_op | source)
XLA Modules:
  0.0 631.7 jit_solution(2216624026873869297)
XLA Ops:
  6.5 0.8 convert_element_type.149
  7.4 3.1 fusion.1
  10.6 5.2 fusion.3
  15.9 2.3 multiply_reduce_fusion.1
  18.1 0.7 fusion.51
  20.5 9.7 %all_to_all.20 = bf16[8,2,1,2048]{3,1,2,0:T(2,128)(2,1)S(1)} all-to-all(bf16[8,2,1,2048]{3,1,2,0:T(2,128)(2,1)S(1)} %bitcast.125), channel_id=1, replica_groups=mesh['req'=8,'exp'=16] {'req'}, dimensions={0} | all-to-all | bytes 131072 | tf_op jit(solution)/shard_map/all_to_all | solution.py:185
  30.9 1.6 gather_fusion
  32.5 13.5 %all_to_all.21 = bf16[8,2,1,32,512]{4,3,1,2,0:T(8,128)(2,1)} all-to-all(bf16[8,2,1,32,512]{4,3,1,2,0:T(8,128)(2,1)S(1)} %bitcast.122), channel_id=1, replica_groups=mesh['req'=8,'exp'=16] {'req'}, dimensions={0} | all-to-all | bytes 1048576 | tf_op jit(solution)/shard_map/all_to_all | solution.py:184
  46.4 1.2 reduce-window.6
  50.6 1.3 fusion.29
  52.1 24.6 %all-gather.1 = bf16[16,65,64]{1,2,0:T(8,128)(2,1)S(1)} all-gather(bf16[1,65,64]{1,2,0:T(8,128)(2,1)S(1)} %maximum_bitcast_fusion), channel_id=1, replica_groups=mesh['req'=8,'exp'=16] {'exp'}, dimensions={0}, use_global_device_ids=true | all-gather | bytes 141440 | tf_op jit(solution)/shard_map/all_gather | solution.py:219
  77.1 3.7 convolution_bitcast_fusion
  81.6 0.7 iota_compare_fusion.7
  82.3 5.3 convolution_convert_fusion.3
  87.6 0.7 slice_bitcast_fusion.2
  88.4 2.4 reshape.471
  90.8 2.3 slice.94
  93.1 0.9 fusion.52
  93.9 14.4 %all-gather.8.cloned.1.call-done = bf16[16,16,2048]{2,0,1:T(8,128)(2,1)} async-done(((bf16[16,1,2048]{2,0,1:T(8,128)(2,1)}), bf16[16,16,2048]{2,0,1:T(8,128)(2,1)}) %all-gather.8.cloned.1.call-update) | async-done | bytes 1048592 | tf_op jit(solution)/shard_map/all_gather | solution.py:191
  108.3 2.8 copy.77
  111.1 5.1 gather_fusion.4
  116.2 4.4 gather.35
  120.6 3.2 broadcast_select_fusion
  123.9 1.4 copy-done.1
  125.4 2.3 fusion.87
  127.6 53.2 %all-gather.6.cloned.1.call-done = bf16[16,16,32,512]{3,2,0,1:T(8,128)(2,1)} async-done(((bf16[16,1,32,512]{3,2,0,1:T(8,128)(2,1)}), bf16[16,16,32,512]{3,2,0,1:T(8,128)(2,1)}) %all-gather.6.cloned.1.call-update) | async-done | bytes 8388624 | tf_op jit(solution)/shard_map/all_gather | solution.py:190
  180.8 13.4 %gather_fusion.3 = bf16[256,32,512]{2,1,0:T(8,128)(2,1)} fusion(bf16[16,16,32,512]{3,2,0,1:T(8,128)(2,1)} %all-gather.6.cloned.1.call-done, s32[256]{0:T(256)S(1)} %reshape.436), kind=kCustom, calls=%fused_computation.3 | custom fusion | bytes 16779264 | tf_op jit(solution)/shard_map/jit(take_along_axis)/gather | solution.py:193
  194.2 4.9 bitcast_select_fusion
  199.2 2.3 fusion.59
  202.0 1.2 fusion.57
  203.5 1.8 fusion.23
  205.3 2.3 fusion.86
  207.6 2.1 fusion.5
  209.7 3.4 fusion.12
  213.1 0.8 fusion.54
  214.0 5.1 convolution_convert_fusion.1
  219.1 66.7 %fusion = bf16[80,2048]{1,0:T(8,128)(2,1)S(1)} fusion(bf16[1040,2048]{1,0:T(8,128)(2,1)} %convolution_convert_fusion.1), kind=kCustom, calls=%all-reduce-scatter | all-reduce-scatter fusion | flops 2621441 | bytes 4588032
  285.8 0.8 slice.109
  286.6 3.7 collective-permute-start.1
  290.4 3.0 collective-permute-start
  293.4 2.7 collective-permute-start.2
  297.8 2.1 collective-permute-done.2
  299.9 3.8 collective-permute-done
  303.7 11.8 %concatenate.48 = bf16[305,2048]{1,0:T(8,128)(2,1)} concatenate(bf16[65,2048]{1,0:T(8,128)(2,1)} %collective-permute-done.2, bf16[80,2048]{1,0:T(8,128)(2,1)} %collective-permute-done.1, bf16[80,2048]{1,0:T(8,128)(2,1)} %collective-permute-done, bf16[80,2048]{1,0:T(8,128)(2,1)S(1)} %fusion), dimensions={0} | concatenate | bytes 2498560
  315.5 1.4 fusion.25
  316.9 2.5 convolution_convert_fusion.2
  319.3 5.4 broadcast_in_dim.120
  324.7 6.8 %broadcast_in_dim.121 = bf16[64,2,10,2048]{3,2,1,0:T(8,128)(2,1)} broadcast(bf16[64,10,2048]{2,1,0:T(8,128)(2,1)} %broadcast_in_dim.120), dimensions={0,2,3} | broadcast | bytes 7864320 | tf_op jit(solution)/shard_map/broadcast_in_dim | solution.py:267
  331.5 114.1 %all_to_all.22 = bf16[128,1,10,2048]{3,2,1,0:T(8,128)(2,1)} all-to-all(bf16[128,1,10,2048]{3,2,1,0:T(8,128)(2,1)} %bitcast.119), channel_id=1, replica_groups=mesh['req'=8,'exp'=16] {'req','exp'}, dimensions={0} | all-to-all | bytes 10485760 | tf_op jit(solution)/shard_map/all_to_all | solution.py:272
  445.5 9.8 %reshape_squeeze.3 = bf16[1280,2048]{1,0:T(8,128)(2,1)} reshape(bf16[128,1,10,2048]{3,2,1,0:T(8,128)(2,1)} %all_to_all.22) | data formatting | bytes 10485760 | tf_op jit(solution)/shard_map/reshape;squeeze | solution.py:135
  455.4 7.4 %fusion.10 = f32[1280,704]{0,1:T(8,128)S(1)} fusion(bf16[1280,2048]{1,0:T(8,128)(2,1)} %reshape_squeeze.3, bf16[1,2048,704]{1,2,0:T(8,128)(2,1)} %param.34), kind=kOutput, calls=%fused_computation.31 | convolution fusion | flops 3690987520 | bytes 11730944 | tf_op jit(solution)/shard_map/dot_general | solution.py:127
  462.8 4.2 fusion.6
  467.1 6.1 convolution_convert_fusion
  473.2 9.5 %stack_reshape.3 = bf16[128,1,10,2048]{3,2,0,1:T(8,128)(2,1)} reshape(bf16[1280,2048]{1,0:T(8,128)(2,1)} %convolution_convert_fusion) | data formatting | bytes 10485760 | tf_op jit(solution)/shard_map/stack;reshape | solution.py:138
  482.7 6.6 %all-to-all-start.3 = ((bf16[128,1,10,2048]{3,2,1,0:T(8,128)(2,1)}), bf16[128,1,10,2048]{3,2,1,0:T(8,128)(2,1)}, u32[]{:S(2)}, u32[]{:S(2)}) async-start(bf16[128,1,10,2048]{3,2,1,0:T(8,128)(2,1)} %bitcast.117), calls=%async_computation.3 | async-start | bytes 16777216 | tf_op jit(solution)/shard_map/all_to_all | solution.py:277
  489.7 1.3 fusion.15
  491.0 4.8 gather_fusion.5
  496.1 102.0 %all-to-all-done.3 = bf16[128,1,10,2048]{3,2,1,0:T(8,128)(2,1)} async-done(((bf16[128,1,10,2048]{3,2,1,0:T(8,128)(2,1)}), bf16[128,1,10,2048]{3,2,1,0:T(8,128)(2,1)}, u32[]{:S(2)}, u32[]{:S(2)}) %all-to-all-start.3) | async-done | bytes 5242912 | tf_op jit(solution)/shard_map/all_to_all | solution.py:277
  598.1 5.7 add_convert_fusion
  603.8 5.5 convert_element_type.181
  609.3 7.2 %gather_fusion.2 = bf16[390,2048]{1,0:T(8,128)(2,1)} fusion(bf16[640,2048]{1,0:T(8,128)(2,1)} %convert_element_type.181, s32[1024]{0:T(1024)S(1)} %pad_clamp_fusion), kind=kCustom, calls=%fused_computation.2 | custom fusion | bytes 3196440 | tf_op jit(solution)/shard_map/gather | solution.py:284
  616.5 3.9 reshape.400
  620.4 3.8 multiply_reduce_fusion
  624.2 0.8 fusion.28
  (105 shorter events, 8.3 us)
Async XLA Ops:
  6.5 460.5 %copy-start = (bf16[1,704,2048]{2,1,0:T(8,128)(2,1)S(1)}, bf16[1,704,2048]{2,1,0:T(8,128)(2,1)}, u32[]{:S(2)}) copy-start(bf16[1,704,2048]{2,1,0:T(8,128)(2,1)} %param.36) | copy-start | bytes 8650756
  6.5 4.0 copy-start.12
  6.5 81.8 %all-gather.10.cloned.1.call-start = ((), (), s32[]{:S(2)}) async-start(), calls=%async_computation.6 | async-start | bytes 1253376 | tf_op jit(solution)/shard_map/all_gather | solution.py:218
  10.6 8.4 %copy-start.15 = (s32[16]{0:T(128)S(1)}, s32[16]{0:T(128)}, u32[]{:S(2)}) copy-start(s32[16]{0:T(128)} %param.40) | copy-start | bytes 196
  10.6 9.2 %copy-start.3 = (bf16[16,1,2048]{2,0,1:T(8,128)(2,1)S(1)}, bf16[16,1,2048]{2,0,1:T(8,128)(2,1)}, u32[]{:S(2)}) copy-start(bf16[16,1,2048]{2,0,1:T(8,128)(2,1)} %param.39) | copy-start | bytes 196612
  15.8 30.2 %copy-start.8 = (s32[65,6]{0,1:T(8,128)S(1)}, s32[65,6]{0,1:T(8,128)}, u32[]{:S(2)}) copy-start(s32[65,6]{0,1:T(8,128)} %param.37) | copy-start | bytes 4684
  15.9 32.3 %copy-start.9 = (s32[16,16]{1,0:T(8,128)S(1)}, s32[16,16]{1,0:T(8,128)}, u32[]{:S(2)}) copy-start(s32[16,16]{1,0:T(8,128)} %param.41) | copy-start | bytes 3076
  15.9 33.3 %copy-start.10 = (s32[16]{0:T(128)S(1)}, s32[16]{0:T(128)}, u32[]{:S(2)}) copy-start(s32[16]{0:T(128)} %param.42) | copy-start | bytes 196
  18.9 89.4 %all-gather.8.cloned.1.call-start = ((), (), s32[]{:S(2)}) async-start(), calls=%async_computation.5 | async-start | bytes 1114112 | tf_op jit(solution)/shard_map/all_gather | solution.py:191
  30.9 149.9 %all-gather.6.cloned.1.call-start = ((), (), s32[]{:S(2)}) async-start(), calls=%async_computation.4 | async-start | bytes 8912896 | tf_op jit(solution)/shard_map/all_gather | solution.py:190
  77.1 10.5 %copy-start.6 = (bf16[1040,64]{0,1:T(8,128)(2,1)}, bf16[1040,64]{0,1:T(8,128)(2,1)S(1)}, u32[]{:S(2)}) copy-start(bf16[1040,64]{0,1:T(8,128)(2,1)S(1)} %reshape.473) | copy-start | bytes 399364
  123.8 1.4 copy-start.1
  201.9 1.2 copy-start.4
  202.0 1.5 copy-start.5
  203.5 1.8 slice-start
  209.7 4.2 copy-start.7
  213.9 82.2 %copy-start.11 = (bf16[2048]{0:T(1024)(128)(2,1)S(1)}, bf16[2048]{0:T(1024)(128)(2,1)}, u32[]{:S(2)}) copy-start(bf16[2048]{0:T(1024)(128)(2,1)} %param.32) | copy-start | bytes 12292
  213.9 82.2 %copy-start.13 = (u32[128]{0:T(128)S(1)}, u32[128]{0:T(128)}, u32[]{:S(2)}) copy-start(u32[128]{0:T(128)} %constant.195) | copy-start | bytes 1540
  286.6 13.3 %collective-permute-start.1 = (bf16[80,2048]{1,0:T(8,128)(2,1)S(1)}, bf16[80,2048]{1,0:T(8,128)(2,1)}, u32[]{:S(2)}, u32[]{:S(2)}) collective-permute-start(bf16[80,2048]{1,0:T(8,128)(2,1)S(1)} %fusion), channel_id=1, source_target_pairs={{0,2},{1,3},{2,4},{3,5},{4,6},{5,7},{6,8},{7,9},{8,10},{9,11},{10,... | collective-permute-start | bytes 983048
  290.4 13.3 %collective-permute-start = (bf16[80,2048]{1,0:T(8,128)(2,1)S(1)}, bf16[80,2048]{1,0:T(8,128)(2,1)}, u32[]{:S(2)}, u32[]{:S(2)}) collective-permute-start(bf16[80,2048]{1,0:T(8,128)(2,1)S(1)} %fusion), channel_id=1, source_target_pairs={{0,1},{1,2},{2,3},{3,4},{4,5},{5,6},{6,7},{7,8},{8,9},{9,10},{10,1... | collective-permute-start | bytes 983048
  293.4 6.5 %collective-permute-start.2 = (bf16[65,2048]{1,0:T(8,128)(2,1)}, bf16[65,2048]{1,0:T(8,128)(2,1)}, u32[]{:S(2)}, u32[]{:S(2)}) collective-permute-start(bf16[65,2048]{1,0:T(8,128)(2,1)} %slice.109), channel_id=1, source_target_pairs={{0,3},{1,4},{2,5},{3,6},{4,7},{5,8},{6,9},{7,10},{8,11},{9,12},{10... | collective-permute-start | bytes 798728
  455.4 7.4 %copy-start.2 = (bf16[1280,2048]{1,0:T(8,128)(2,1)S(1)}, bf16[1280,2048]{1,0:T(8,128)(2,1)}, u32[]{:S(2)}) copy-start(bf16[1280,2048]{1,0:T(8,128)(2,1)} %reshape_squeeze.3) | copy-start | bytes 15728644
  455.4 7.5 %copy-start.14 = (bf16[1,2048,704]{1,2,0:T(8,128)(2,1)S(1)}, bf16[1,2048,704]{1,2,0:T(8,128)(2,1)}, u32[]{:S(2)}) copy-start(bf16[1,2048,704]{1,2,0:T(8,128)(2,1)} %param.35) | copy-start | bytes 8650756
  482.7 115.4 %all-to-all-start.3 = ((bf16[128,1,10,2048]{3,2,1,0:T(8,128)(2,1)}), bf16[128,1,10,2048]{3,2,1,0:T(8,128)(2,1)}, u32[]{:S(2)}, u32[]{:S(2)}) async-start(bf16[128,1,10,2048]{3,2,1,0:T(8,128)(2,1)} %bitcast.117), calls=%async_computation.3 | async-start | bytes 16777216 | tf_op jit(solution)/shard_map/all_to_all | solution.py:277
Sparse Core Ops, SparseCore 0:
  19.0 44.8 all-gather.9
  66.1 42.1 all-gather.7
  110.4 70.2 all-gather.5
where the time goes:
time: 641 us; the launch traced here: 632 us
  blocking collectives  229 us (36%)
  waiting for transfers between devices  175 us (27%)
  local copies, waits for them, and re-layouts  105 us (16%)
  matrix products  52.4 us (8%)
  other arithmetic  38.1 us (6%)
  starting transfers between devices  16.1 us (3%)
  between operations  15.9 us (2%)
    all_to_all x1, blocking collectives, shards(): lax.all_to_all(doubled, ('req', 'exp'), split_axis=0, concat_axis=0, tile...  114 us
    all_to_all x1, waiting for transfers between devices, shards(): lax.all_to_all(computed, ('req', 'exp'), split_axis=0, concat_axis=0, til...  102 us
    unnamed x1, blocking collectives  66.7 us
    all_gather x1, waiting for transfers between devices, shards(): lax.all_gather(local_latent, 'exp', axis=1, tiled=True)  53.2 us
    all_gather x1, blocking collectives, shards(): lax.all_gather(own_rope, 'exp', axis=0, tiled=True)  24.6 us
    unnamed x38, local copies, waits for them, and re-layouts  17.8 us
    all_gather x1, waiting for transfers between devices, shards(): lax.all_gather(local_rope, 'exp', axis=1, tiled=True)  14.4 us
    gather x2, local copies, waits for them, and re-layouts, shards(): jnp.take_along_axis(whole_latent, page_table[:, :, None, None], axis=1)  13.5 us
  transfers between devices with their start and end apart: 7, of which 5 were waited for; matrix products, arithmetic and copies ran while one was open for 8% of the time, Pallas kernels for 0%

commit v1 on v0

v1 whole, which is shorter than its diff:
```python
import functools
import math

import jax
import jax.numpy as jnp
from jax import lax
from jax.experimental import pallas as pl
from jax.experimental.pallas import tpu as pltpu
from jax.sharding import PartitionSpec as P

DN = 128
DR = 64
RANK = 512
KEY = RANK + DR
TOP = 6
SPAN = 1024
LANES = 128
F32 = jnp.float32
BF16 = jnp.bfloat16
MIB = 1 << 20

theta_base = 50000.0
route_scale = 2.446
norm_eps = 1e-06


def rms_scale(values, gain_values):
    widened = values.astype(F32)
    mean_square = jnp.mean(widened * widened, axis=-1, keepdims=True)
    return widened * lax.rsqrt(mean_square + norm_eps) * gain_values.astype(F32)


def rope_angles(positions, rope_width):
    exponent = jnp.arange(rope_width // 2, dtype=F32) * (2.0 / rope_width)
    frequency = jnp.exp(-exponent * math.log(theta_base))
    return positions.astype(F32)[:, None] * frequency[None, :]


def rotate(values, cosine, sine):
    half = values.shape[-1] // 2
    first, second = values[..., :half], values[..., half:]
    return jnp.concatenate(
        [first * cosine - second * sine, second * cosine + first * sine], axis=-1
    )


def dot(a, b):
    return jnp.dot(a, b, preferred_element_type=F32)


def dot_t(a, b):
    return lax.dot_general(a, b, (((1,), (1,)), ((), ())), preferred_element_type=F32)


def whole(shape):
    return pl.BlockSpec(shape, lambda *_: (0,) * len(shape))


def pack_kernel(table, rows_ref, out_ref, padded):
    experts, _, cap = out_ref.shape[:3]
    count = rows_ref.shape[0]
    padded[0:count] = rows_ref[...]
    padded[count] = jnp.zeros(padded.shape[1:], padded.dtype)
    first = pl.program_id(0) * experts

    def one(e, carry):
        for c in range(cap):
            row = padded[table[(first + e) * cap + c]]
            out_ref[e, 0, c] = row
            out_ref[e, 1, c] = row
        return carry

    lax.fori_loop(0, experts, one, 0)


def pack_rows(table, rows, experts, cap):
    count, blocks, lanes = rows.shape
    step = 8
    return pl.pallas_call(
        pack_kernel,
        grid_spec=pltpu.PrefetchScalarGridSpec(
            num_scalar_prefetch=1,
            grid=(experts // step,),
            in_specs=[pl.BlockSpec((count, blocks, lanes), lambda i, t: (0, 0, 0))],
            out_specs=pl.BlockSpec(
                (step, 2, cap, blocks, lanes), lambda i, t: (i, 0, 0, 0, 0)
            ),
            scratch_shapes=[pltpu.VMEM((count + 1, blocks, lanes), rows.dtype)],
        ),
        out_shape=jax.ShapeDtypeStruct((experts, 2, cap, blocks, lanes), rows.dtype),
        compiler_params=pltpu.CompilerParams(vmem_limit_bytes=32 * MIB),
    )(table, rows)


def combine_kernel(slots, gates, half_ref, resid_ref, out_ref):
    cap = half_ref.shape[1]

    def one(t, carry):
        total = resid_ref[t].astype(F32)
        mixed = jnp.zeros_like(total)
        for k in range(TOP):
            slot = slots[t * TOP + k]
            expert = slot // cap
            place = slot - expert * cap
            both = half_ref[2 * expert, place].astype(F32) + half_ref[
                2 * expert + 1, place
            ].astype(F32)
            mixed = mixed + gates[t * TOP + k] * both.astype(BF16).astype(F32)
        out_ref[t] = (total + mixed).astype(BF16)
        return carry

    lax.fori_loop(0, out_ref.shape[0], one, 0)


def combine_rows(slots, gates, halves, resid):
    return pl.pallas_call(
        combine_kernel,
        grid_spec=pltpu.PrefetchScalarGridSpec(
            num_scalar_prefetch=2,
            grid=(1,),
            in_specs=[
                pl.BlockSpec(halves.shape, lambda i, s, g: (0, 0, 0, 0)),
                pl.BlockSpec(resid.shape, lambda i, s, g: (0, 0, 0)),
            ],
            out_specs=pl.BlockSpec(resid.shape, lambda i, s, g: (0, 0, 0)),
        ),
        out_shape=jax.ShapeDtypeStruct(resid.shape, BF16),
        compiler_params=pltpu.CompilerParams(vmem_limit_bytes=32 * MIB),
    )(slots, gates, halves, resid)


def expert_kernel(x_ref, gate_ref, up_ref, down_ref, out_ref, wide, lhs):
    blocks = x_ref.shape[1]
    wide[...] = x_ref[...].astype(F32)
    for c in range(blocks):
        lhs[:, c * LANES : (c + 1) * LANES] = wide[:, c, :].astype(BF16)
    x = lhs[...]
    hidden_gate = dot(x, gate_ref[0])
    hidden_up = dot(x, up_ref[0])
    hidden = (hidden_gate / (1.0 + jnp.exp(-hidden_gate)) * hidden_up).astype(BF16)
    step = 4 * LANES
    for n in range(0, blocks * LANES, step):
        part = dot(hidden, down_ref[0, :, n : n + step]).astype(BF16).astype(F32)
        for c in range(step // LANES):
            wide[:, n // LANES + c, :] = part[:, c * LANES : (c + 1) * LANES]
    out_ref[...] = wide[...].astype(BF16)


def expert_rows(x, w_gate, w_up, w_down):
    rows, blocks, lanes = x.shape
    step = 320
    resident = functools.partial(pl.BlockSpec, pipeline_mode=pl.Buffered(1))
    return pl.pallas_call(
        expert_kernel,
        grid=(rows // step,),
        in_specs=[
            pl.BlockSpec((step, blocks, lanes), lambda i: (i, 0, 0)),
            resident(w_gate.shape, lambda i: (0, 0, 0)),
            resident(w_up.shape, lambda i: (0, 0, 0)),
            resident(w_down.shape, lambda i: (0, 0, 0)),
        ],
        out_specs=pl.BlockSpec((step, blocks, lanes), lambda i: (i, 0, 0)),
        out_shape=jax.ShapeDtypeStruct(x.shape, BF16),
        scratch_shapes=[
            pltpu.VMEM((step, blocks, lanes), F32),
            pltpu.VMEM((step, blocks * lanes), BF16),
        ],
        compiler_params=pltpu.CompilerParams(vmem_limit_bytes=48 * MIB),
    )(x, w_gate, w_up, w_down)


def softmax_rows(scores, visible):
    masked = jnp.where(visible, scores, -jnp.inf)
    row_top = jnp.max(masked, axis=-1, keepdims=True)
    raised = jnp.where(visible, jnp.exp(masked - row_top), 0.0)
    return (raised / jnp.sum(raised, axis=-1, keepdims=True)).astype(BF16)


def block_positions(page_row, page_size):
    pages = page_row.shape[0]
    ids = jnp.arange(pages, dtype=jnp.int32)
    logical = jnp.sum(
        jnp.where(page_row[:, None] == ids[None, :], ids[:, None], 0), axis=0
    )
    inside = jnp.arange(page_size, dtype=jnp.int32)
    return (logical[:, None] * page_size + inside[None, :]).reshape(-1)


def shards(
    tokens,
    attn_gain,
    wq_nope,
    wq_rope,
    w_latent,
    w_krope,
    latent_gain,
    w_uk,
    w_uv,
    w_out,
    moe_gain,
    w_router,
    w_gate,
    w_up,
    w_down,
    routes,
    cache_latent,
    cache_rope,
    mig_dest,
    page_table,
    cache_len,
    span_slot,
):
    req_count = lax.axis_size("req")
    exp_count = lax.axis_size("exp")
    device_count = req_count * exp_count
    own_exp = lax.axis_index("exp")
    req_group = mig_dest.shape[0]
    move_count = req_group // req_count
    page_size = cache_latent.shape[2]
    rows_group, width = tokens.shape
    rows_device = rows_group // exp_count
    blocks = width // LANES
    scale_factor = 1.0 / math.sqrt(DN + DR)

    w_out_all = lax.all_gather(w_out, "exp", axis=0, tiled=True)

    expert_count = w_router.shape[1]
    capacity = 2 * ((rows_device * TOP // expert_count + 5) // 2)
    expert_ids = jnp.arange(expert_count, dtype=jnp.int32)
    named = routes[:, :, None] == expert_ids[None, None, :]
    member = jnp.any(named, axis=1)
    row_ids = jnp.arange(rows_device, dtype=jnp.int32)
    before = (row_ids[None, :] < row_ids[:, None]).astype(BF16)
    rank = dot(before, member.astype(BF16)).astype(jnp.int32)
    slot_of = jnp.sum(
        jnp.where(named, rank[:, None, :] + expert_ids[None, None, :] * capacity, 0), axis=2
    )
    place_ids = jnp.arange(capacity, dtype=jnp.int32)
    filled = member[:, :, None] & (rank[:, :, None] == place_ids[None, None, :])
    table = rows_device + jnp.sum(
        jnp.where(filled, row_ids[:, None, None] - rows_device, 0), axis=0
    )

    slot_ids = jnp.arange(req_group, dtype=jnp.int32)
    earlier = (mig_dest[None, :] == mig_dest[:, None]) & (slot_ids[None, :] < slot_ids[:, None])
    placed = mig_dest * move_count + jnp.sum(earlier.astype(jnp.int32), axis=1)
    order = (placed[None, :] == slot_ids[:, None]).astype(BF16)
    pages = jnp.concatenate(
        [cache_latent[:, 0], cache_rope.reshape(req_group, page_size, DR)], axis=2
    )
    outgoing = jnp.einsum("os,sik->oik", order, pages, preferred_element_type=F32).astype(BF16)
    arrived = lax.all_to_all(
        outgoing.reshape(req_count, move_count * page_size, KEY),
        "req",
        split_axis=0,
        concat_axis=0,
        tiled=True,
    ).reshape(req_group, page_size, KEY)

    normed = rms_scale(tokens, attn_gain).astype(BF16)
    span_len = lax.dynamic_index_in_dim(cache_len, span_slot[0], 0, keepdims=False)
    positions = jnp.concatenate([span_len + jnp.arange(SPAN, dtype=jnp.int32), cache_len])
    angles = rope_angles(positions, DR)
    cosine, sine = jnp.cos(angles), jnp.sin(angles)
    query_nope = dot(normed, wq_nope).astype(BF16)
    query_rope = rotate(dot(normed, wq_rope), cosine, sine).astype(BF16)
    query = jnp.concatenate([dot_t(query_nope, w_uk).astype(BF16), query_rope], axis=1)
    new_keys = jnp.concatenate(
        [
            rms_scale(dot(normed, w_latent), latent_gain).astype(BF16),
            rotate(dot(normed, w_krope), cosine, sine).astype(BF16),
        ],
        axis=1,
    )

    span_page = lax.dynamic_index_in_dim(arrived, span_slot[0], 0)
    message = jnp.concatenate(
        [
            jnp.broadcast_to(span_page, arrived.shape),
            arrived,
            query[SPAN:, None, :],
            jnp.zeros((req_group, 7, KEY), BF16),
        ],
        axis=1,
    )
    message = lax.all_to_all(message, "exp", split_axis=0, concat_axis=0, tiled=True)
    span_cache = message[:, :page_size].reshape(-1, KEY)
    own_cache = message[:, page_size : 2 * page_size].reshape(-1, KEY)
    own_query = message[:, 2 * page_size]

    own_len = lax.dynamic_index_in_dim(cache_len, own_exp, 0, keepdims=False)
    own_pages = lax.dynamic_index_in_dim(page_table, own_exp, 0, keepdims=False)
    own_key = lax.dynamic_slice_in_dim(new_keys, SPAN + own_exp, 1, 0)
    own_seen = block_positions(own_pages, page_size) < own_len
    own_scores = dot_t(own_query, own_cache) * scale_factor
    self_score = (
        jnp.sum(own_query.astype(F32) * own_key.astype(F32), axis=1, keepdims=True) * scale_factor
    )
    own_masked = jnp.where(own_seen[None, :], own_scores, -jnp.inf)
    own_top = jnp.maximum(jnp.max(own_masked, axis=1, keepdims=True), self_score)
    own_raised = jnp.where(own_seen[None, :], jnp.exp(own_masked - own_top), 0.0)
    self_raised = jnp.exp(self_score - own_top)
    own_total = jnp.sum(own_raised, axis=1, keepdims=True) + self_raised
    own_out = (
        dot((own_raised / own_total).astype(BF16), own_cache[:, :RANK])
        + (self_raised / own_total).astype(BF16).astype(F32) * own_key[:, :RANK].astype(F32)
    ).astype(BF16)
    decode_out = lax.all_to_all(
        own_out[:, None, :], "exp", split_axis=0, concat_axis=0, tiled=True
    )[:, 0]

    span_table = lax.dynamic_index_in_dim(page_table, span_slot[0], 0, keepdims=False)
    span_seen = block_positions(span_table, page_size) < span_len
    key_ids = jnp.arange(SPAN, dtype=jnp.int32)
    keys = jnp.concatenate([span_cache, new_keys[:SPAN]], axis=0)
    visible = jnp.concatenate(
        [
            jnp.broadcast_to(span_seen[None, :], (SPAN, span_seen.shape[0])),
            key_ids[None, :] <= key_ids[:, None],
        ],
        axis=1,
    )
    weights = softmax_rows(dot_t(query[:SPAN], keys) * scale_factor, visible)
    span_out = dot(weights, keys[:, :RANK]).astype(BF16)
    attended = jnp.concatenate([span_out, decode_out], axis=0)
    head_out = dot(attended, w_uv).astype(BF16)

    heads_in = lax.all_to_all(
        head_out.reshape(exp_count, rows_device, DN),
        "exp",
        split_axis=0,
        concat_axis=0,
        tiled=True,
    )
    own_heads = jnp.transpose(heads_in, (1, 0, 2)).reshape(rows_device, width)
    own_tokens = lax.dynamic_slice_in_dim(tokens, own_exp * rows_device, rows_device, 0)
    resid = (own_tokens.astype(F32) + dot(own_heads, w_out_all)).astype(BF16)
    moe_in = rms_scale(resid, moe_gain).astype(BF16)
    scores = jax.nn.sigmoid(dot(moe_in, w_router))
    picked = jnp.sum(jnp.where(named, scores[:, None, :], 0.0), axis=2)
    gate_w = route_scale * picked / jnp.sum(picked, axis=1, keepdims=True)

    packed = pack_rows(
        table.reshape(-1),
        moe_in.reshape(rows_device, blocks, LANES),
        expert_count,
        capacity,
    )
    received = lax.all_to_all(
        packed.reshape(device_count, capacity * blocks, LANES),
        ("req", "exp"),
        split_axis=0,
        concat_axis=0,
        tiled=True,
    )
    computed = expert_rows(
        received.reshape(device_count * capacity, blocks, LANES), w_gate, w_up, w_down
    )
    returned = lax.all_to_all(
        computed.reshape(device_count, capacity * blocks, LANES),
        ("req", "exp"),
        split_axis=0,
        concat_axis=0,
        tiled=True,
    )
    mixed = combine_rows(
        slot_of.reshape(-1),
        gate_w.reshape(-1),
        returned.reshape(device_count, capacity, blocks, LANES),
        resid.reshape(rows_device, blocks, LANES),
    )
    return mixed.reshape(rows_device, width)


def solution(mesh):
    in_specs = (
        P("req", None),
        P(),
        P(None, "exp"),
        P(None, "exp"),
        P(),
        P(),
        P(),
        P(None, "exp"),
        P(None, "exp"),
        P("exp", None),
        P(),
        P(),
        P(("req", "exp"), None, None),
        P(("req", "exp"), None, None),
        P(("req", "exp"), None, None),
        P(("req", "exp"), None),
        P("req", "exp", None, None),
        P("req", "exp", None),
        P("req"),
        P("req", None),
        P("req"),
        P("req"),
    )
    out_specs = P(("req", "exp"), None)
    return jax.shard_map(shards, mesh=mesh, in_specs=in_specs, out_specs=out_specs, check_vma=False)
```

time: 641 us -> 339 us (0.53); the launches traced: 632 us -> 337 us
  blocking collectives: 229 us -> 0 us
  local copies, waits for them, and re-layouts: 105 us -> 30.9 us
  Pallas kernels: 0 us -> 40.4 us
  starting transfers between devices: 16.1 us -> 42.6 us
  matrix products: 52.4 us -> 28.9 us
  waiting for transfers between devices: 175 us -> 158 us
  other arithmetic: 38.1 us -> 21.7 us
    all_to_all x3 -> x0, blocking collectives: 137 us -> none  [the longest x1 114 us: shards(): lax.all_to_all(doubled, ('req', 'exp'), split_axis=0, concat_axis=0, tile...]
    all_gather x3 -> x1, waiting for transfers between devices: 67.5 us -> 0.02 us  [shards(): w_out_all = lax.all_gather(w_out, 'exp', axis=0, tiled=True)]
    unnamed x1 -> x0, blocking collectives: 66.7 us -> none
    all_to_all x1 -> x6, waiting for transfers between devices: 102 us -> 157 us  [the longest x1 65.1 us: shards(): lax.all_to_all(computed.reshape(device_count, capacity * blocks, LANES),...]
    pallas_call x0 -> x3, Pallas kernels: none -> 40.4 us  [the longest x1 31.4 us: expert_rows(): pl.pallas_call(expert_kernel, grid=(rows // step,), in_specs=[pl.BlockSpe...]
    gather x12 -> x0, local copies, waits for them, and re-layouts: 37.7 us -> none  [the longest x2 13.5 us: shards(): jnp.take_along_axis(whole_latent, page_table[:, :, None, None], axis=1)]
    all_to_all x1 -> x6, starting transfers between devices: 6.57 us -> 42.6 us  [the longest x1 9.46 us: shards(): lax.all_to_all(own_out[:, None, :], 'exp', split_axis=0, concat_axis=0, t...]
    all_gather x1 -> x0, blocking collectives: 24.6 us -> none  [shards(): lax.all_gather(own_rope, 'exp', axis=0, tiled=True)]
  transfers between devices with their start and end apart: 7 -> 7, of which waited for: 5 -> 4; matrix products, arithmetic and copies ran while one was open for 8% -> 20% of each run, Pallas kernels for 0% -> 0%
where the time goes in v1:
time: 339 us; the launch traced here: 337 us
  waiting for transfers between devices  158 us (47%)
  starting transfers between devices  42.6 us (13%)
  Pallas kernels  40.4 us (12%)
  local copies, waits for them, and re-layouts  30.9 us (9%)
  matrix products  28.9 us (9%)
  other arithmetic  21.7 us (6%)
  between operations  14.8 us (4%)
    all_to_all x1, waiting for transfers between devices, shards(): lax.all_to_all(computed.reshape(device_count, capacity * blocks, LANES),...  65.1 us
    all_to_all x1, waiting for transfers between devices, shards(): lax.all_to_all(packed.reshape(device_count, capacity * blocks, LANES), ('...  56.9 us
    pallas_call x1, Pallas kernels, expert_rows(): pl.pallas_call(expert_kernel, grid=(rows // step,), in_specs=[pl.BlockSpe...  31.4 us
    all_to_all x1, waiting for transfers between devices, shards(): lax.all_to_all(message, 'exp', split_axis=0, concat_axis=0, tiled=True)  28.8 us
    dot_general x9, matrix products, dot(): return jnp.dot(a, b, preferred_element_type=F32)  19.6 us
    unnamed x62, local copies, waits for them, and re-layouts  18.9 us
    all_to_all x1, starting transfers between devices, shards(): lax.all_to_all(own_out[:, None, :], 'exp', split_axis=0, concat_axis=0, t...  9.46 us
    dot_general x3, matrix products, dot_t(): lax.dot_general(a, b, (((1,), (1,)), ((), ())), preferred_element_type=F32)  8.94 us
  transfers between devices with their start and end apart: 7, of which 4 were waited for; matrix products, arithmetic and copies ran while one was open for 20% of the time, Pallas kernels for 0%

profile of v1, /device:TPU:32, one launch (start us, length us, event | category | flops | bytes accessed | tf_op | source)
XLA Modules:
  0.0 337.4 jit_solution(11961765367491100539)
XLA Ops:
  6.5 0.7 all-gather.2.cloned.1.call-update
  7.3 1.0 reshape.204
  8.4 1.3 copy.148
  9.7 0.9 convert_reduce_fusion
  10.6 0.7 multiply_add_fusion
  11.3 0.3 convolution_convert_fusion.3
  11.6 1.0 copy.123
  12.6 4.3 %all-to-all-start = ((bf16[8,64,576]{2,1,0:T(8,128)(2,1)}), bf16[8,64,576]{2,1,0:T(8,128)(2,1)}, u32[]{:S(2)}, u32[]{:S(2)}) async-start(bf16[8,64,576]{2,1,0:T(8,128)(2,1)} %bitcast.5), calls=%async_computation | async-start | bytes 1310720 | tf_op jit(solution)/shard_map/all_to_all | solution.py:252
  17.6 0.7 fusion.74
  18.2 1.0 iota_add_fusion
  19.3 3.3 fusion
  22.6 1.0 fusion.2
  23.7 1.4 fusion.77
  25.1 0.5 copy-done.5
  25.6 1.4 fusion.76
  27.1 0.7 fusion.49
  27.7 0.2 copy.120
  28.1 0.8 fusion.61
  29.1 6.0 %multiply_reduce_fusion = (f32[1040]{0:T(1024)S(1)}, f32[1040,512]{1,0:T(8,128)}) fusion(bf16[1040,2048]{1,0:T(8,128)(2,1)} %copy-done.5, bf16[2048,512]{1,0:T(8,128)(2,1)S(1)} %copy-done), kind=kOutput, calls=%fused_computation.19 | convolution fusion | flops 2182102016 | bytes 8491072 | tf_op jit(solution)/shard_map/dot_general | solution.py:48
  35.2 4.2 %convolution_convert_fusion = bf16[1040,512]{1,0:T(8,128)(2,1)S(1)} fusion(bf16[512,128]{1,0:T(8,128)(2,1)S(1)} %copy-done.18, bf16[1040,2048]{1,0:T(8,128)(2,1)} %copy-done.5, bf16[2048,128]{1,0:T(8,128)(2,1)S(1)} %copy-done.14), kind=kOutput, calls=%fused_computation.13 | convolution fusion | flops 682240000 | bytes 5980160 | tf_op jit(solution)/shard_map/dot_general | solution.py:52
  39.3 2.9 multiply_convert_fusion
  42.6 0.2 copy.125
  42.8 0.7 add_compare_fusion.1
  43.6 1.4 pad_maximum_fusion.1
  45.0 0.8 dynamic-slice_bitcast_fusion
  45.9 2.6 maximum_maximum_fusion
  48.5 8.7 %all-to-all-start.1 = ((bf16[16,72,576]{2,1,0:T(8,128)(2,1)}), bf16[16,72,576]{2,1,0:T(8,128)(2,1)}, u32[]{:S(2)}, u32[]{:S(2)}) async-start(bf16[16,72,576]{2,1,0:T(8,128)(2,1)} %maximum_maximum_fusion), calls=%async_computation.1 | async-start | bytes 2949120 | tf_op jit(solution)/shard_map/all_to_all | solution.py:286
  57.2 0.6 add_compare_fusion
  57.9 1.2 slice.58
  59.3 0.3 iota_compare_fusion
  59.8 1.3 pad_maximum_fusion
  61.1 28.8 %all-to-all-done.1 = bf16[16,72,576]{2,1,0:T(8,128)(2,1)} async-done(((bf16[16,72,576]{2,1,0:T(8,128)(2,1)}), bf16[16,72,576]{2,1,0:T(8,128)(2,1)}, u32[]{:S(2)}, u32[]{:S(2)}) %all-to-all-start.1) | async-done | bytes 1327136 | tf_op jit(solution)/shard_map/all_to_all | solution.py:286
  89.9 0.9 slice.59
  90.9 2.2 fusion.73
  93.2 0.4 fusion.75
  93.6 0.2 fusion.52
  93.8 0.2 fusion.23
  94.0 0.5 broadcast.166
  94.5 0.7 reduce.3
  95.2 0.6 reshape.223
  95.8 9.5 %all-to-all-start.2 = ((bf16[16,2,256]{2,1,0:T(2,128)(2,1)}), bf16[16,2,256]{2,1,0:T(2,128)(2,1)S(1)}, u32[]{:S(2)}, u32[]{:S(2)}) async-start(bf16[16,2,256]{2,1,0:T(2,128)(2,1)} %reshape.223), calls=%async_computation.2 | async-start | bytes 32768 | tf_op jit(solution)/shard_map/all_to_all | solution.py:308
  105.3 4.4 %fusion.3 = (f32[1024]{0:T(1024)S(1)}, f32[1024,1536]{1,0:T(8,128)S(1)}) fusion(pred[1024,1024]{1,0:T(32,128)(4,1)S(1)} %iota_compare_fusion, pred[1536]{0:T(1024)(128)(4,1)S(1)} %pad.18.clone, bf16[1024,576]{1,0:T(8,128)(2,1)} %slice.58, bf16[512,576]{1,0:T(8,128)(2,1)} %bitcast.85, bf16[1040,576]{1,0:T(8,128)(2,1)S(1)} %copy-done.11), kind=kOutput, calls=%fused_computation.9 | convolution fusion | flops 1821768704 | bytes 10426368 | tf_op jit(solution)/shard_map/dot_general | solution.py:52
  109.7 2.4 fusion.4
  112.1 3.3 fusion.14
  115.5 1.7 convolution_convert_fusion.1
  117.2 0.8 reshape.209
  118.0 7.2 %all-to-all-start.3 = ((bf16[16,65,128]{2,1,0:T(8,128)(2,1)}), bf16[16,65,128]{2,1,0:T(8,128)(2,1)S(1)}, u32[]{:S(2)}, u32[]{:S(2)}) async-start(bf16[16,65,128]{2,1,0:T(8,128)(2,1)} %reshape.209), calls=%async_computation.3 | async-start | bytes 589824 | tf_op jit(solution)/shard_map/all_to_all | solution.py:328
  125.2 0.2 select_reduce_fusion
  125.7 6.6 %all-to-all-done.3 = bf16[16,65,128]{2,1,0:T(8,128)(2,1)S(1)} async-done(((bf16[16,65,128]{2,1,0:T(8,128)(2,1)}), bf16[16,65,128]{2,1,0:T(8,128)(2,1)S(1)}, u32[]{:S(2)}, u32[]{:S(2)}) %all-to-all-start.3) | async-done | bytes 266272 | tf_op jit(solution)/shard_map/all_to_all | solution.py:328
  132.5 5.1 %fusion.30 = (f32[65]{0:T(128)S(1)}, bf16[65,2048]{1,0:T(8,128)(2,1)S(1)}) fusion(bf16[65,2048]{1,0:T(8,128)(2,1)S(1)} %bitcast.79, bf16[2048,2048]{1,0:T(8,128)(2,1)} %all-gather.2.cloned.1.call-done, bf16[1040,2048]{1,0:T(8,128)(2,1)} %param.22, s32[]{:T(128)S(6)} %select_n.52), kind=kOutput, calls=%fused_computation.51 | convolution fusion | flops 546058176 | bytes 9187592 | tf_op jit(solution)/shard_map/dot_general | solution.py:48
  137.9 2.2 shard_map.208
  140.1 2.3 copy-done.2
  142.5 8.2 %all-to-all-start.4 = ((bf16[128,160,128]{2,1,0:T(8,128)(2,1)}), bf16[128,160,128]{2,1,0:T(8,128)(2,1)}, u32[]{:S(2)}, u32[]{:S(2)}) async-start(bf16[128,160,128]{2,1,0:T(8,128)(2,1)} %bitcast.72), calls=%async_computation.4 | async-start | bytes 10485760 | tf_op jit(solution)/shard_map/all_to_all | solution.py:349
  150.6 4.6 %copy.132.gate_ref = bf16[1,2048,704]{2,1,0:T(8,128)(2,1)} copy(bf16[1,2048,704]{1,2,0:T(8,128)(2,1)} %param.34) | data formatting | bytes 5767168 | tf_op args[12]
  155.3 4.7 %copy.133.up_ref = bf16[1,2048,704]{2,1,0:T(8,128)(2,1)} copy(bf16[1,2048,704]{1,2,0:T(8,128)(2,1)} %param.35) | data formatting | bytes 5767168 | tf_op args[13]
  159.9 56.9 %all-to-all-done.4 = bf16[128,160,128]{2,1,0:T(8,128)(2,1)} async-done(((bf16[128,160,128]{2,1,0:T(8,128)(2,1)}), bf16[128,160,128]{2,1,0:T(8,128)(2,1)}, u32[]{:S(2)}, u32[]{:S(2)}) %all-to-all-start.4) | async-done | bytes 5242912 | tf_op jit(solution)/shard_map/all_to_all | solution.py:349
  216.8 1.9 copy-done.3
  218.7 1.8 copy-done.4
  220.5 31.4 %shard_map.209 = bf16[1280,16,128]{2,1,0:T(8,128)(2,1)} custom-call(bf16[1280,16,128]{2,1,0:T(8,128)(2,1)} %bitcast.18.x_ref, bf16[1,2048,704]{2,1,0:T(8,128)(2,1)S(1)} %copy-done.3, bf16[1,2048,704]{2,1,0:T(8,128)(2,1)} %copy.133.up_ref, bf16[1,704,2048]{2,1,0:T(8,128)(2,1)S(1)} %copy-done.4), custom_call_target="tpu_custom_call" | custom-call | tf_op jit(solution)/shard_map/pallas_call | solution.py:153
  251.9 4.9 %all-to-all-start.5 = ((bf16[128,160,128]{2,1,0:T(8,128)(2,1)}), bf16[128,160,128]{2,1,0:T(8,128)(2,1)}, u32[]{:S(2)}, u32[]{:S(2)}) async-start(bf16[128,160,128]{2,1,0:T(8,128)(2,1)} %bitcast.73), calls=%async_computation.5 | async-start | bytes 10485760 | tf_op jit(solution)/shard_map/all_to_all | solution.py:359
  257.1 0.2 fusion.21
  257.8 65.1 %all-to-all-done.5 = bf16[128,160,128]{2,1,0:T(8,128)(2,1)} async-done(((bf16[128,160,128]{2,1,0:T(8,128)(2,1)}), bf16[128,160,128]{2,1,0:T(8,128)(2,1)}, u32[]{:S(2)}, u32[]{:S(2)}) %all-to-all-start.5) | async-done | bytes 5242912 | tf_op jit(solution)/shard_map/all_to_all | solution.py:359
  322.9 6.8 %shard_map.210 = bf16[65,16,128]{2,1,0:T(8,128)(2,1)S(1)} custom-call(s32[390]{0:T(512)S(1)} %reshape.203.slots, f32[390]{0:T(512)S(1)} %div.71.gates, bf16[128,10,16,128]{3,2,1,0:T(8,128)(2,1)} %bitcast.20.half_ref, bf16[65,16,128]{2,1,0:T(8,128)(2,1)S(1)} %slice.63.resid_ref), custom_call_target="tpu_custom_call" | custom-call | tf_op jit(solution)/shard_map/pallas_call | solution.py:116
  329.7 0.8 copy.139
  (102 shorter events, 2.7 us)
Async XLA Ops:
  6.5 22.5 %copy-start = (bf16[2048,512]{1,0:T(8,128)(2,1)S(1)}, bf16[2048,512]{1,0:T(8,128)(2,1)}, u32[]{:S(2)}) copy-start(bf16[2048,512]{1,0:T(8,128)(2,1)} %param.26) | copy-start | bytes 6291460
  6.5 125.9 %all-gather.2.cloned.1.call-start = ((), (), s32[]{:S(2)}) async-start(), calls=%async_computation.6 | async-start | bytes 8912896 | tf_op jit(solution)/shard_map/all_gather | solution.py:225
  8.3 8.6 %copy-start.21 = (bf16[2048]{0:T(1024)(128)(2,1)S(1)}, bf16[2048]{0:T(1024)(128)(2,1)}, u32[]{:S(2)}) copy-start(bf16[2048]{0:T(1024)(128)(2,1)} %param.23) | copy-start | bytes 12292
  8.3 9.3 %copy-start.20 = (s32[16]{0:T(128)S(1)}, s32[16]{0:T(128)}, u32[]{:S(2)}) copy-start(s32[16]{0:T(128)} %param.42) | copy-start | bytes 196
  12.6 32.4 %all-to-all-start = ((bf16[8,64,576]{2,1,0:T(8,128)(2,1)}), bf16[8,64,576]{2,1,0:T(8,128)(2,1)}, u32[]{:S(2)}, u32[]{:S(2)}) async-start(bf16[8,64,576]{2,1,0:T(8,128)(2,1)} %bitcast.5), calls=%async_computation | async-start | bytes 1310720 | tf_op jit(solution)/shard_map/all_to_all | solution.py:252
  17.6 5.0 %copy-start.6 = (bf16[1040,2048]{1,0:T(8,128)(2,1)S(1)}, bf16[1040,2048]{1,0:T(8,128)(2,1)}, u32[]{:S(2)}) copy-start(bf16[1040,2048]{1,0:T(8,128)(2,1)} %param.22) | copy-start | bytes 12779524
  22.6 1.1 copy-start.15
  23.6 2.0 copy-start.5
  23.6 2.0 copy-start.16
  25.6 2.5 copy-start.23
  27.9 14.3 %copy-start.7 = (bf16[1040,32]{1,0:T(8,128)(2,1)}, bf16[1040,32]{1,0:T(8,128)(2,1)S(1)}, u32[]{:S(2)}) copy-start(bf16[1040,32]{1,0:T(8,128)(2,1)S(1)} %copy.120) | copy-start | bytes 199684
  28.1 14.1 %copy-start.9 = (bf16[1040,32]{1,0:T(8,128)(2,1)}, bf16[1040,32]{1,0:T(8,128)(2,1)S(1)}, u32[]{:S(2)}) copy-start(bf16[1040,32]{1,0:T(8,128)(2,1)S(1)} %copy.119) | copy-start | bytes 199684
  29.1 6.1 %copy-start.14 = (bf16[2048,128]{1,0:T(8,128)(2,1)S(1)}, bf16[2048,128]{1,0:T(8,128)(2,1)}, u32[]{:S(2)}) copy-start(bf16[2048,128]{1,0:T(8,128)(2,1)} %param.24) | copy-start | bytes 1572868
  29.1 6.1 %copy-start.18 = (bf16[512,128]{1,0:T(8,128)(2,1)S(1)}, bf16[512,128]{1,0:T(8,128)(2,1)}, u32[]{:S(2)}) copy-start(bf16[512,128]{1,0:T(8,128)(2,1)} %param.29) | copy-start | bytes 393220
  48.5 10.8 %copy-start.19 = (s32[65,6]{0,1:T(8,128)S(1)}, s32[65,6]{0,1:T(8,128)}, u32[]{:S(2)}) copy-start(s32[65,6]{0,1:T(8,128)} %param.37) | copy-start | bytes 4684
  48.5 11.3 %copy-start.8 = (bf16[1040,32]{1,0:T(8,128)(2,1)S(1)}, bf16[1040,32]{1,0:T(8,128)(2,1)}, u32[]{:S(2)}) copy-start(bf16[1040,32]{1,0:T(8,128)(2,1)} %copy-done.7) | copy-start | bytes 199684
  48.5 11.3 %copy-start.10 = (bf16[1040,32]{1,0:T(8,128)(2,1)S(1)}, bf16[1040,32]{1,0:T(8,128)(2,1)}, u32[]{:S(2)}) copy-start(bf16[1040,32]{1,0:T(8,128)(2,1)} %copy-done.9) | copy-start | bytes 199684
  48.5 41.3 %all-to-all-start.1 = ((bf16[16,72,576]{2,1,0:T(8,128)(2,1)}), bf16[16,72,576]{2,1,0:T(8,128)(2,1)}, u32[]{:S(2)}, u32[]{:S(2)}) async-start(bf16[16,72,576]{2,1,0:T(8,128)(2,1)} %maximum_maximum_fusion), calls=%async_computation.1 | async-start | bytes 2949120 | tf_op jit(solution)/shard_map/all_to_all | solution.py:286
  61.1 44.2 %copy-start.11 = (bf16[1040,576]{1,0:T(8,128)(2,1)S(1)}, bf16[1040,576]{1,0:T(8,128)(2,1)}, u32[]{:S(2)}) copy-start(bf16[1040,576]{1,0:T(8,128)(2,1)} %pad_maximum_fusion) | copy-start | bytes 3594244
  95.8 19.7 %all-to-all-start.2 = ((bf16[16,2,256]{2,1,0:T(2,128)(2,1)}), bf16[16,2,256]{2,1,0:T(2,128)(2,1)S(1)}, u32[]{:S(2)}, u32[]{:S(2)}) async-start(bf16[16,2,256]{2,1,0:T(2,128)(2,1)} %reshape.223), calls=%async_computation.2 | async-start | bytes 32768 | tf_op jit(solution)/shard_map/all_to_all | solution.py:308
  109.7 2.4 copy-start.12
  109.7 2.4 copy-start.13
  112.1 3.4 %copy-start.24 = (bf16[512,128]{1,0:T(8,128)(2,1)S(1)}, bf16[512,128]{1,0:T(8,128)(2,1)}, u32[]{:S(2)}) copy-start(bf16[512,128]{1,0:T(8,128)(2,1)} %param.30) | copy-start | bytes 393220
  115.5 10.0 %copy-start.22 = (bf16[2048]{0:T(1024)(128)(2,1)S(1)}, bf16[2048]{0:T(1024)(128)(2,1)}, u32[]{:S(2)}) copy-start(bf16[2048]{0:T(1024)(128)(2,1)} %param.32) | copy-start | bytes 12292
  118.0 14.3 %all-to-all-start.3 = ((bf16[16,65,128]{2,1,0:T(8,128)(2,1)}), bf16[16,65,128]{2,1,0:T(8,128)(2,1)S(1)}, u32[]{:S(2)}, u32[]{:S(2)}) async-start(bf16[16,65,128]{2,1,0:T(8,128)(2,1)} %reshape.209), calls=%async_computation.3 | async-start | bytes 589824 | tf_op jit(solution)/shard_map/all_to_all | solution.py:328
  140.1 2.3 copy-start.2
  142.5 74.4 %all-to-all-start.4 = ((bf16[128,160,128]{2,1,0:T(8,128)(2,1)}), bf16[128,160,128]{2,1,0:T(8,128)(2,1)}, u32[]{:S(2)}, u32[]{:S(2)}) async-start(bf16[128,160,128]{2,1,0:T(8,128)(2,1)} %bitcast.72), calls=%async_computation.4 | async-start | bytes 10485760 | tf_op jit(solution)/shard_map/all_to_all | solution.py:349
  216.8 1.9 copy-start.3
  218.7 1.8 copy-start.4
  251.9 5.2 %copy-start.17 = (bf16[2048,64]{0,1:T(8,128)(2,1)S(1)}, bf16[2048,64]{0,1:T(8,128)(2,1)}, u32[]{:S(2)}) copy-start(bf16[2048,64]{0,1:T(8,128)(2,1)} %param.33) | copy-start | bytes 786436
  251.9 71.0 %all-to-all-start.5 = ((bf16[128,160,128]{2,1,0:T(8,128)(2,1)}), bf16[128,160,128]{2,1,0:T(8,128)(2,1)}, u32[]{:S(2)}, u32[]{:S(2)}) async-start(bf16[128,160,128]{2,1,0:T(8,128)(2,1)} %bitcast.73), calls=%async_computation.5 | async-start | bytes 10485760 | tf_op jit(solution)/shard_map/all_to_all | solution.py:359
  322.9 7.6 %copy-start.1 = (bf16[2048,512]{1,0:T(8,128)(2,1)S(1)}, bf16[2048,512]{1,0:T(8,128)(2,1)}, u32[]{:S(2)}) copy-start(bf16[2048,512]{1,0:T(8,128)(2,1)} %param.26) | copy-start | bytes 6291460
Sparse Core Ops, SparseCore 0:
  9.5 88.5 all-gather.1

commit v2 on v1

v2 whole, which is shorter than its diff:
```python
import functools
import math

import jax
import jax.numpy as jnp
from jax import lax
from jax.experimental import pallas as pl
from jax.experimental.pallas import tpu as pltpu
from jax.sharding import PartitionSpec as P

DN = 128
DR = 64
RANK = 512
KEY = RANK + DR
TOP = 6
SPAN = 1024
LANES = 128
REQ = ("x", "core")
FLAT = ("x", "core", "exp")
F32 = jnp.float32
BF16 = jnp.bfloat16
MIB = 1 << 20

theta_base = 50000.0
route_scale = 2.446
norm_eps = 1e-06


def rms_scale(values, gain_values):
    widened = values.astype(F32)
    mean_square = jnp.mean(widened * widened, axis=-1, keepdims=True)
    return widened * lax.rsqrt(mean_square + norm_eps) * gain_values.astype(F32)


def rope_angles(positions, rope_width):
    exponent = jnp.arange(rope_width // 2, dtype=F32) * (2.0 / rope_width)
    frequency = jnp.exp(-exponent * math.log(theta_base))
    return positions.astype(F32)[:, None] * frequency[None, :]


def rotate(values, cosine, sine):
    half = values.shape[-1] // 2
    first, second = values[..., :half], values[..., half:]
    return jnp.concatenate(
        [first * cosine - second * sine, second * cosine + first * sine], axis=-1
    )


def dot(a, b):
    return jnp.dot(a, b, preferred_element_type=F32)


def dot_t(a, b):
    return lax.dot_general(a, b, (((1,), (1,)), ((), ())), preferred_element_type=F32)


def whole(shape):
    return pl.BlockSpec(shape, lambda *_: (0,) * len(shape))


def pack_kernel(table, rows_ref, out_ref, padded, made, sems):
    experts, _, cap = made.shape[:3]
    count = rows_ref.shape[0]
    parts = sems.shape[0]
    step = experts // parts
    padded[0:count] = rows_ref[...]
    padded[count] = jnp.zeros(padded.shape[1:], padded.dtype)

    def part_copy(p):
        piece = pl.ds(p * step, step)
        return pltpu.make_async_copy(made.at[piece], out_ref.at[piece], sems.at[p])

    for p in range(parts):

        def one(e, carry):
            for c in range(cap):
                row = padded[table[e * cap + c]]
                made[e, 0, c] = row
                made[e, 1, c] = row
            return carry

        lax.fori_loop(p * step, (p + 1) * step, one, 0)
        part_copy(p).start()
    for p in range(parts):
        part_copy(p).wait()


def pack_rows(table, rows, experts, cap):
    count, blocks, lanes = rows.shape
    shape = (experts, 2, cap, blocks, lanes)
    return pl.pallas_call(
        pack_kernel,
        in_specs=[
            pl.BlockSpec(memory_space=pltpu.SMEM),
            pl.BlockSpec(memory_space=pltpu.VMEM),
        ],
        out_specs=pl.BlockSpec(memory_space=pl.ANY),
        scratch_shapes=[
            pltpu.VMEM((count + 1, blocks, lanes), rows.dtype),
            pltpu.VMEM(shape, rows.dtype),
            pltpu.SemaphoreType.DMA((8,)),
        ],
        out_shape=jax.ShapeDtypeStruct(shape, rows.dtype),
        compiler_params=pltpu.CompilerParams(vmem_limit_bytes=60 * MIB),
    )(table, rows)


def combine_kernel(slots, gates, half_ref, resid_ref, out_ref):
    cap = half_ref.shape[2]

    def one(t, carry):
        total = resid_ref[t].astype(F32)
        mixed = jnp.zeros_like(total)
        for k in range(TOP):
            slot = slots[t * TOP + k]
            expert = slot // cap
            place = slot - expert * cap
            both = half_ref[expert, 0, place].astype(F32) + half_ref[expert, 1, place].astype(F32)
            mixed = mixed + gates[t * TOP + k] * both.astype(BF16).astype(F32)
        out_ref[t] = (total + mixed).astype(BF16)
        return carry

    lax.fori_loop(0, out_ref.shape[0], one, 0, unroll=5)


def combine_rows(slots, gates, halves, resid):
    return pl.pallas_call(
        combine_kernel,
        grid_spec=pltpu.PrefetchScalarGridSpec(
            num_scalar_prefetch=2,
            grid=(1,),
            in_specs=[
                pl.BlockSpec(halves.shape, lambda i, s, g: (0, 0, 0, 0, 0)),
                pl.BlockSpec(resid.shape, lambda i, s, g: (0, 0, 0)),
            ],
            out_specs=pl.BlockSpec(resid.shape, lambda i, s, g: (0, 0, 0)),
        ),
        out_shape=jax.ShapeDtypeStruct(resid.shape, BF16),
        compiler_params=pltpu.CompilerParams(vmem_limit_bytes=32 * MIB),
    )(slots, gates, halves, resid)


def expert_kernel(x_ref, gate_hbm, up_hbm, down_hbm, out_ref, gate_ref, up_ref, down_ref, sems):
    copies = [
        pltpu.make_async_copy(source, target, sems.at[i])
        for i, (source, target) in enumerate(
            ((gate_hbm, gate_ref), (up_hbm, up_ref), (down_hbm, down_ref))
        )
    ]
    opening = pl.program_id(0) == 0

    @pl.when(opening)
    def _():
        for copy in copies:
            copy.start()
        copies[0].wait()
        copies[1].wait()

    rows, blocks, lanes = x_ref.shape
    x = x_ref[...].reshape(rows, blocks * lanes)
    hidden_gate = dot_t(x, gate_ref[0])
    hidden_up = dot_t(x, up_ref[0])
    hidden = (hidden_gate / (1.0 + jnp.exp(-hidden_gate)) * hidden_up).astype(BF16)

    @pl.when(opening)
    def _():
        copies[2].wait()

    step = 4
    for n in range(0, blocks, step):
        part = dot(hidden, down_ref[0, :, n * lanes : (n + step) * lanes]).astype(BF16)
        out_ref[:, n : n + step, :] = part.reshape(rows, step, lanes)


def expert_rows(x, weights):
    rows, blocks, lanes = x.shape
    step = 320
    return pl.pallas_call(
        expert_kernel,
        grid=(rows // step,),
        in_specs=[pl.BlockSpec((step, blocks, lanes), lambda i: (i, 0, 0))]
        + [pl.BlockSpec(memory_space=pl.ANY)] * 3,
        out_specs=pl.BlockSpec((step, blocks, lanes), lambda i: (i, 0, 0)),
        out_shape=jax.ShapeDtypeStruct((rows, blocks, lanes), BF16),
        scratch_shapes=[pltpu.VMEM(w.shape, w.dtype) for w in weights]
        + [pltpu.SemaphoreType.DMA((3,))],
        compiler_params=pltpu.CompilerParams(vmem_limit_bytes=60 * MIB),
        cost_estimate=pl.CostEstimate(
            flops=6 * rows * blocks * lanes * weights[0].shape[1],
            bytes_accessed=4 * rows * blocks * lanes,
            transcendentals=rows * weights[0].shape[1],
        ),
    )(x, *weights)


def project_kernel(
    tokens_ref,
    gain_ref,
    nope_ref,
    rope_ref,
    krope_ref,
    latent_ref,
    latent_gain_ref,
    uk_ref,
    cos_ref,
    sin_ref,
    query_ref,
    key_ref,
    turned,
):
    @pl.when(pl.program_id(0) == 0)
    def _():
        turned[:DR] = rope_ref[...]
        turned[DR:] = krope_ref[...]

    normed = rms_scale(tokens_ref[...], gain_ref[...]).astype(BF16)
    cosine, sine = cos_ref[...], sin_ref[...]

    def turn(v):
        half = DR // 2
        swapped = jnp.concatenate([v[:, half:], v[:, :half]], axis=1)
        return (v * cosine + swapped * sine).astype(BF16)

    ropes = dot_t(normed, turned[...])
    query_ref[:, RANK:] = turn(ropes[:, :DR])
    key_ref[:, RANK:] = turn(ropes[:, DR:])
    nope = dot(normed, nope_ref[...]).astype(BF16)
    query_ref[:, :RANK] = dot_t(nope, uk_ref[...]).astype(BF16)
    latent = dot(normed, latent_ref[...])
    key_ref[:, :RANK] = rms_scale(latent, latent_gain_ref[...]).astype(BF16)


def project(tokens, gain, nope, rope, krope, latent, latent_gain, uk, cosine, sine):
    rows, width = tokens.shape
    step = 208
    fixed = (gain, nope, rope, krope, latent, latent_gain, uk)
    return pl.pallas_call(
        project_kernel,
        grid=(rows // step,),
        in_specs=[pl.BlockSpec((step, width), lambda i: (i, 0))]
        + [
            pl.BlockSpec(a.shape, lambda i: (0, 0), pipeline_mode=pl.Buffered(1))
            for a in fixed
        ]
        + [pl.BlockSpec((step, DR), lambda i: (i, 0))] * 2,
        out_specs=[pl.BlockSpec((step, KEY), lambda i: (i, 0))] * 2,
        out_shape=[jax.ShapeDtypeStruct((rows, KEY), BF16)] * 2,
        scratch_shapes=[pltpu.VMEM((2 * DR, width), BF16)],
        compiler_params=pltpu.CompilerParams(vmem_limit_bytes=32 * MIB),
        cost_estimate=pl.CostEstimate(
            flops=2 * rows * width * (DN + 2 * DR + RANK),
            bytes_accessed=2 * rows * (width + 2 * KEY) + 2 * width * (DN + 2 * DR + RANK),
            transcendentals=0,
        ),
    )(tokens, *fixed, cosine, sine)


def decode_kernel(scale, message_ref, key_ref, seen_ref, out_ref):
    page = message_ref.shape[1] // 9 * 4
    query = message_ref[:, 2 * page, :]
    cache = message_ref[:, page : 2 * page, :].reshape(-1, KEY)
    own = key_ref[...].astype(F32)
    scores = dot_t(query, cache) * scale + seen_ref[...]
    self_score = jnp.sum(query.astype(F32) * own, axis=1, keepdims=True) * scale
    top = jnp.maximum(jnp.max(scores, axis=1, keepdims=True), self_score)
    raised = jnp.exp(scores - top)
    self_raised = jnp.exp(self_score - top)
    total = jnp.sum(raised, axis=1, keepdims=True) + self_raised
    out_ref[...] = (
        dot((raised / total).astype(BF16), cache[:, :RANK])
        + (self_raised / total).astype(BF16).astype(F32) * own[:, :RANK]
    ).astype(BF16)


def decode(message, own_key, seen, scale):
    heads = message.shape[0]
    return pl.pallas_call(
        functools.partial(decode_kernel, scale),
        out_shape=jax.ShapeDtypeStruct((heads, RANK), BF16),
        compiler_params=pltpu.CompilerParams(vmem_limit_bytes=16 * MIB),
        cost_estimate=pl.CostEstimate(
            flops=1 << 25, bytes_accessed=1 << 21, transcendentals=1 << 13
        ),
    )(message, own_key, seen)


def attend_kernel(scale, query_ref, message_ref, new_ref, seen_ref, uv_ref, out_ref):
    step = query_ref.shape[0]
    first = pl.program_id(0) * step
    query = query_ref[...]
    old = message_ref[...].reshape(-1, KEY)
    new = new_ref[...]
    old_scores = dot_t(query, old) * scale + seen_ref[...]
    new_scores = dot_t(query, new) * scale
    rows = lax.broadcasted_iota(jnp.int32, new_scores.shape, 0) + first
    keys = lax.broadcasted_iota(jnp.int32, new_scores.shape, 1)
    new_scores = jnp.where(keys <= rows, new_scores, -jnp.inf)
    top = jnp.maximum(
        jnp.max(old_scores, axis=1, keepdims=True), jnp.max(new_scores, axis=1, keepdims=True)
    )
    old_raised = jnp.exp(old_scores - top)
    new_raised = jnp.exp(new_scores - top)
    total = jnp.sum(old_raised, axis=1, keepdims=True) + jnp.sum(
        new_raised, axis=1, keepdims=True
    )
    share = 1.0 / total
    attended = dot((old_raised * share).astype(BF16), old[:, :RANK]) + dot(
        (new_raised * share).astype(BF16), new[:, :RANK]
    )
    out_ref[...] = dot(attended.astype(BF16), uv_ref[...]).astype(BF16)


def attend(query, message, new, seen, uv, scale):
    step = 256
    pages = message.shape[0]
    page = seen.shape[1] // pages

    def once(shape):
        zeros = (0,) * len(shape)
        return pl.BlockSpec(shape, lambda i: zeros, pipeline_mode=pl.Buffered(1))

    return pl.pallas_call(
        functools.partial(attend_kernel, scale),
        grid=(SPAN // step,),
        in_specs=[
            pl.BlockSpec((step, KEY), lambda i: (i, 0)),
            once((pages, page, KEY)),
            once((SPAN, KEY)),
            once(seen.shape),
            once(uv.shape),
        ],
        out_specs=pl.BlockSpec((step, uv.shape[1]), lambda i: (i, 0)),
        out_shape=jax.ShapeDtypeStruct((SPAN, uv.shape[1]), BF16),
        compiler_params=pltpu.CompilerParams(vmem_limit_bytes=32 * MIB),
        cost_estimate=pl.CostEstimate(
            flops=4 * SPAN * (SPAN + seen.shape[1]) * KEY,
            bytes_accessed=1 << 22,
            transcendentals=SPAN * (SPAN + seen.shape[1]),
        ),
    )(query, message, new, seen, uv)


def after(values):
    return values[(0,) * values.ndim].astype(F32) * 0.0


def seen_bias(page_row, page_size, length):
    pages = page_row.shape[0]
    ids = jnp.arange(pages, dtype=jnp.int32)
    logical = jnp.sum(
        jnp.where(page_row[:, None] == ids[None, :], ids[:, None], 0), axis=0
    )
    inside = jnp.arange(page_size, dtype=jnp.int32)
    position = (logical[:, None] * page_size + inside[None, :]).reshape(1, -1)
    return jnp.where(position < length, 0.0, -jnp.inf).astype(F32)


def shards(
    tokens,
    attn_gain,
    wq_nope,
    wq_rope,
    w_latent,
    w_krope,
    latent_gain,
    w_uk,
    w_uv,
    w_out,
    moe_gain,
    w_router,
    w_gate,
    w_up,
    w_down,
    routes,
    cache_latent,
    cache_rope,
    mig_dest,
    page_table,
    cache_len,
    span_slot,
):
    req_count = lax.axis_size(REQ)
    exp_count = lax.axis_size("exp")
    device_count = req_count * exp_count
    own_exp = lax.axis_index("exp")
    req_group = mig_dest.shape[0]
    move_count = req_group // req_count
    page_size = cache_latent.shape[2]
    rows_group, width = tokens.shape
    rows_device = rows_group // exp_count
    blocks = width // LANES
    scale_factor = 1.0 / math.sqrt(DN + DR)

    half_width = width // 2
    own_core = lax.axis_index("core")
    w_out_half = lax.all_gather(
        lax.dynamic_slice_in_dim(w_out, own_core * half_width, half_width, 1),
        "exp",
        axis=0,
        tiled=True,
    )

    expert_count = w_router.shape[1]
    capacity = 2 * ((rows_device * TOP // expert_count + 5) // 2)
    expert_ids = jnp.arange(expert_count, dtype=jnp.int32)
    named = routes[:, :, None] == expert_ids[None, None, :]
    member = jnp.any(named, axis=1)
    row_ids = jnp.arange(rows_device, dtype=jnp.int32)
    before = (row_ids[None, :] < row_ids[:, None]).astype(BF16)
    rank = dot(before, member.astype(BF16)).astype(jnp.int32)
    slot_of = jnp.sum(
        jnp.where(named, rank[:, None, :] + expert_ids[None, None, :] * capacity, 0), axis=2
    )
    place_ids = jnp.arange(capacity, dtype=jnp.int32)
    filled = member[:, :, None] & (rank[:, :, None] == place_ids[None, None, :])
    table = rows_device + jnp.sum(
        jnp.where(filled, row_ids[:, None, None] - rows_device, 0), axis=0
    )

    slot_ids = jnp.arange(req_group, dtype=jnp.int32)
    earlier = (mig_dest[None, :] == mig_dest[:, None]) & (slot_ids[None, :] < slot_ids[:, None])
    placed = mig_dest * move_count + jnp.sum(earlier.astype(jnp.int32), axis=1)
    order = (placed[None, :] == slot_ids[:, None]).astype(BF16)
    pages = jnp.concatenate(
        [cache_latent[:, 0], cache_rope.reshape(req_group, page_size, DR)], axis=2
    )
    outgoing = jnp.einsum("os,sik->oik", order, pages, preferred_element_type=F32).astype(BF16)
    arrived = lax.all_to_all(
        outgoing.reshape(req_count, move_count * page_size, KEY),
        REQ,
        split_axis=0,
        concat_axis=0,
        tiled=True,
    ).reshape(req_group, page_size, KEY)

    span_len = lax.dynamic_index_in_dim(cache_len, span_slot[0], 0, keepdims=False)
    positions = jnp.concatenate([span_len + jnp.arange(SPAN, dtype=jnp.int32), cache_len])
    angles = rope_angles(positions, DR)
    cosine, sine = jnp.cos(angles), jnp.sin(angles)
    late_cosine, late_sine = cosine[SPAN:], sine[SPAN:]
    late = rms_scale(tokens[SPAN:], attn_gain).astype(BF16)
    late_query = jnp.concatenate(
        [
            dot_t(dot(late, wq_nope).astype(BF16), w_uk).astype(BF16),
            rotate(dot(late, wq_rope), late_cosine, late_sine).astype(BF16),
        ],
        axis=1,
    )

    span_page = lax.dynamic_index_in_dim(arrived, span_slot[0], 0)
    message = jnp.concatenate(
        [
            jnp.broadcast_to(span_page, arrived.shape),
            arrived,
            late_query[:, None, :],
            jnp.zeros((req_group, 7, KEY), BF16),
        ],
        axis=1,
    )
    query, new_keys = project(
        tokens,
        (attn_gain + after(message).astype(BF16))[None, :],
        wq_nope,
        wq_rope.T,
        w_krope.T,
        w_latent,
        latent_gain[None, :],
        w_uk,
        jnp.concatenate([cosine, cosine], axis=1),
        jnp.concatenate([-sine, sine], axis=1),
    )

    message = lax.all_to_all(message, "exp", split_axis=0, concat_axis=0, tiled=True)
    own_len = lax.dynamic_index_in_dim(cache_len, own_exp, 0, keepdims=False)
    own_pages = lax.dynamic_index_in_dim(page_table, own_exp, 0, keepdims=False)
    own_key = lax.dynamic_slice_in_dim(new_keys, SPAN + own_exp, 1, 0)
    own_out = decode(
        message, own_key, seen_bias(own_pages, page_size, own_len), scale_factor
    )
    decode_out = lax.all_to_all(
        own_out[:, None, :], "exp", split_axis=0, concat_axis=0, tiled=True
    )[:, 0]

    span_table = lax.dynamic_index_in_dim(page_table, span_slot[0], 0, keepdims=False)
    span_out = attend(
        query, message, new_keys, seen_bias(span_table, page_size, span_len), w_uv, scale_factor
    )
    head_out = jnp.concatenate([span_out, dot(decode_out, w_uv).astype(BF16)], axis=0)

    heads_in = lax.all_to_all(
        jnp.broadcast_to(
            head_out.reshape(1, exp_count, rows_device, DN), (2, exp_count, rows_device, DN)
        ).reshape(2 * exp_count, rows_device, DN),
        ("core", "exp"),
        split_axis=0,
        concat_axis=0,
        tiled=True,
    ).reshape(2, exp_count, rows_device, DN)
    chip_heads = jnp.transpose(heads_in, (0, 2, 1, 3)).reshape(2 * rows_device, width)
    chip_half = dot(chip_heads, w_out_half).reshape(2, rows_device, half_width)
    own_half = jnp.where(own_core == 0, chip_half[0], chip_half[1])
    other_half = lax.ppermute(
        jnp.where(own_core == 0, chip_half[1], chip_half[0]), "core", [(0, 1), (1, 0)]
    )
    projected = jnp.concatenate(
        [
            jnp.where(own_core == 0, own_half, other_half),
            jnp.where(own_core == 0, other_half, own_half),
        ],
        axis=1,
    )
    own_tokens = lax.dynamic_slice_in_dim(tokens, own_exp * rows_device, rows_device, 0)
    resid = (own_tokens.astype(F32) + projected).astype(BF16)
    moe_in = rms_scale(resid, moe_gain).astype(BF16)
    scores = jax.nn.sigmoid(dot(moe_in, w_router))
    picked = jnp.sum(jnp.where(named, scores[:, None, :], 0.0), axis=2)
    gate_w = route_scale * picked / jnp.sum(picked, axis=1, keepdims=True)

    def spread(rows):
        return lax.all_to_all(
            rows.reshape(device_count, capacity * blocks, LANES),
            FLAT,
            split_axis=0,
            concat_axis=0,
            tiled=True,
        )

    received = spread(
        pack_rows(
            table.reshape(-1),
            moe_in.reshape(rows_device, blocks, LANES),
            expert_count,
            capacity,
        )
    )
    computed = expert_rows(
        received.reshape(device_count * capacity, blocks, LANES),
        (jnp.swapaxes(w_gate, 1, 2), jnp.swapaxes(w_up, 1, 2), w_down),
    )
    mixed = combine_rows(
        slot_of.reshape(-1),
        gate_w.reshape(-1),
        spread(computed).reshape(expert_count, 2, capacity, blocks, LANES),
        resid.reshape(rows_device, blocks, LANES),
    )
    return mixed.reshape(rows_device, width)


def solution(mesh):
    devices = mesh.devices
    split = jax.sharding.Mesh(
        devices.reshape(devices.shape[0] // 2, 2, devices.shape[1]), FLAT
    )
    in_specs = (
        P(REQ, None),
        P(),
        P(None, "exp"),
        P(None, "exp"),
        P(),
        P(),
        P(),
        P(None, "exp"),
        P(None, "exp"),
        P("exp", None),
        P(),
        P(),
        P(FLAT, None, None),
        P(FLAT, None, None),
        P(FLAT, None, None),
        P(FLAT, None),
        P(REQ, "exp", None, None),
        P(REQ, "exp", None),
        P(REQ),
        P(REQ, None),
        P(REQ),
        P(REQ),
    )
    out_specs = P(FLAT, None)
    return jax.shard_map(
        shards, mesh=split, in_specs=in_specs, out_specs=out_specs, check_vma=False
    )
```

time: 339 us -> 308 us (0.909)
  blocking collectives: 0 us -> 70.3 us
  waiting for transfers between devices: 158 us -> 96.9 us
  matrix products: 28.9 us -> 6 us
  local copies, waits for them, and re-layouts: 30.9 us -> 21.6 us
  other arithmetic: 21.7 us -> 13.6 us
  starting transfers between devices: 42.6 us -> 36.9 us
  Pallas kernels: 40.4 us -> 45.7 us
    all_to_all x0 -> x1, blocking collectives: none -> 70.3 us  [spread(): lax.all_to_all(rows.reshape(device_count, capacity * blocks, LANES), FLAT...]
    all_to_all x3 -> x2, waiting for transfers between devices: 129 us -> 76.5 us  [the longest x1 65.6 us: spread(): lax.all_to_all(rows.reshape(device_count, capacity * blocks, LANES), FLAT...]
    pallas_call x1 -> x4, Pallas kernels: 2.25 us -> 19.1 us  [the longest x1 7.65 us: project(): pl.pallas_call(project_kernel, grid=(rows // step,), in_specs=[pl.BlockSp...]
    dot_general x9 -> x5, matrix products: 19.6 us -> 4.47 us  [dot(): return jnp.dot(a, b, preferred_element_type=F32)]
    all_to_all x1, waiting for transfers between devices: 28.8 us -> 14.8 us  [shards(): lax.all_to_all(message, 'exp', split_axis=0, concat_axis=0, tiled=True)]
    pallas_call x1, Pallas kernels: 31.4 us -> 20.5 us  [expert_rows(): pl.pallas_call(expert_kernel, grid=(rows // step,), in_specs=[pl.BlockSpe...]
    dot_general x3 -> x1, matrix products: 8.94 us -> 1.21 us  [dot_t(): lax.dot_general(a, b, (((1,), (1,)), ((), ())), preferred_element_type=F32)]
    unnamed x62 -> x49, local copies, waits for them, and re-layouts: 18.9 us -> 12.9 us
  transfers between devices with their start and end apart: 7 -> 7, of which waited for: 4 -> 5; matrix products, arithmetic and copies ran while one was open for 20% -> 8% of each run, Pallas kernels for 0% -> 5%
where the time goes in v2:
time: 308 us; the launch traced here: 306 us
  waiting for transfers between devices  96.9 us (31%)
  blocking collectives  70.3 us (23%)
  Pallas kernels  45.7 us (15%)
  starting transfers between devices  36.9 us (12%)
  local copies, waits for them, and re-layouts  21.6 us (7%)
  between operations  15.3 us (5%)
  other arithmetic  13.6 us (4%)
  matrix products  6 us (2%)
    all_to_all x1, blocking collectives, spread(): lax.all_to_all(rows.reshape(device_count, capacity * blocks, LANES), FLAT...  70.3 us
    all_to_all x1, waiting for transfers between devices, spread(): lax.all_to_all(rows.reshape(device_count, capacity * blocks, LANES), FLAT...  65.6 us
    pallas_call x1, Pallas kernels, expert_rows(): pl.pallas_call(expert_kernel, grid=(rows // step,), in_specs=[pl.BlockSpe...  20.5 us
    all_to_all x1, waiting for transfers between devices, shards(): lax.all_to_all(message, 'exp', split_axis=0, concat_axis=0, tiled=True)  14.8 us
    unnamed x49, local copies, waits for them, and re-layouts  12.9 us
    all_to_all x1, waiting for transfers between devices, shards(): lax.all_to_all(jnp.broadcast_to(head_out.reshape(1, exp_count, rows_devic...  10.9 us
    all_to_all x1, starting transfers between devices, shards(): lax.all_to_all(own_out[:, None, :], 'exp', split_axis=0, concat_axis=0, t...  9.07 us
    all_to_all x1, starting transfers between devices, shards(): lax.all_to_all(message, 'exp', split_axis=0, concat_axis=0, tiled=True)  8.19 us
  transfers between devices with their start and end apart: 7, of which 5 were waited for; matrix products, arithmetic and copies ran while one was open for 8% of the time, Pallas kernels for 5%

profile of v2, /device:TPU:32, one launch (start us, length us, event | category | flops | bytes accessed | tf_op | source)
XLA Modules:
  0.0 306.4 jit_solution(12366790260807793962)
XLA Ops:
  6.5 1.0 copy-done
  7.6 0.7 constant_dynamic-slice_fusion
  8.3 1.0 reshape.208
  9.4 1.3 copy.89
  10.8 0.9 convert_reduce_fusion
  11.7 0.7 multiply_add_fusion
  12.4 0.3 convolution_convert_fusion
  12.7 1.0 copy.71
  13.6 4.3 %all-to-all-start = ((bf16[8,64,576]{2,1,0:T(8,128)(2,1)}), bf16[8,64,576]{2,1,0:T(8,128)(2,1)S(1)}, u32[]{:S(2)}, u32[]{:S(2)}) async-start(bf16[8,64,576]{2,1,0:T(8,128)(2,1)} %bitcast.2), calls=%async_computation | async-start | bytes 1310720 | tf_op jit(solution)/shard_map/all_to_all | solution.py:428
  18.7 0.6 fusion.32
  19.3 0.7 fusion.28
  20.0 0.5 iota_add_fusion
  20.7 1.0 fusion.13
  21.7 2.9 fusion.12
  24.6 5.1 %all-to-all-done = bf16[8,64,576]{2,1,0:T(8,128)(2,1)S(1)} async-done(((bf16[8,64,576]{2,1,0:T(8,128)(2,1)}), bf16[8,64,576]{2,1,0:T(8,128)(2,1)S(1)}, u32[]{:S(2)}, u32[]{:S(2)}) %all-to-all-start) | async-done | bytes 589856 | tf_op jit(solution)/shard_map/all_to_all | solution.py:428
  29.7 0.6 slice.37
  31.0 1.1 fusion.23
  32.2 1.2 convolution_convert_fusion.2
  33.6 1.6 maximum_maximum_fusion
  35.2 8.2 %all-to-all-start.1 = ((bf16[16,72,576]{2,1,0:T(8,128)(2,1)}), bf16[16,72,576]{2,1,0:T(8,128)(2,1)S(1)}, u32[]{:S(2)}, u32[]{:S(2)}) async-start(bf16[16,72,576]{2,1,0:T(8,128)(2,1)} %maximum_maximum_fusion), calls=%async_computation.1 | async-start | bytes 2949120 | tf_op jit(solution)/shard_map/all_to_all | solution.py:473
  43.4 0.6 fusion.21
  44.1 0.7 fusion.22
  44.9 1.9 pad_maximum_fusion
  46.8 2.2 copy-done.4
  49.0 1.7 copy-done.7
  50.6 7.6 %shard_map.208 = (bf16[1040,576]{1,0:T(8,128)(2,1)S(1)}, bf16[1040,576]{1,0:T(8,128)(2,1)S(1)}) custom-call(bf16[1040,2048]{1,0:T(8,128)(2,1)S(1)} %copy-done.4, bf16[1,2048]{1,0:T(2,128)(2,1)S(1)} %broadcast_in_dim.126.gain_ref, bf16[2048,128]{1,0:T(8,128)(2,1)S(1)} %copy-done.1, bf16[64,2048]{1,0:T(8,128)(2,1)S(1)} %bitcast.64, ...), custom_call_target="tpu_custom_call" | custom-call | flops 3271557120 | bytes 9801728 | tf_op jit(solution)/shard_map/pallas_call | solution.py:237
  58.3 1.1 copy-done.10
  59.4 1.1 copy-done.5
  60.5 14.8 %all-to-all-done.1.message_ref = bf16[16,72,576]{2,1,0:T(8,128)(2,1)S(1)} async-done(((bf16[16,72,576]{2,1,0:T(8,128)(2,1)}), bf16[16,72,576]{2,1,0:T(8,128)(2,1)S(1)}, u32[]{:S(2)}, u32[]{:S(2)}) %all-to-all-start.1) | async-done | bytes 1327136 | tf_op jit(solution)/shard_map/all_to_all | solution.py:473
  75.3 0.6 shard_map.210
  75.9 0.6 broadcast.168
  76.5 0.7 reduce.1
  77.2 0.6 reshape.222
  77.8 9.1 %all-to-all-start.2 = ((bf16[16,2,256]{2,1,0:T(2,128)(2,1)}), bf16[16,2,256]{2,1,0:T(2,128)(2,1)S(1)}, u32[]{:S(2)}, u32[]{:S(2)}) async-start(bf16[16,2,256]{2,1,0:T(2,128)(2,1)} %reshape.222), calls=%async_computation.2 | async-start | bytes 32768 | tf_op jit(solution)/shard_map/all_to_all | solution.py:480
  86.9 1.3 copy-done.6
  88.2 1.3 copy-done.11
  89.6 7.4 %shard_map.209 = bf16[1024,128]{1,0:T(8,128)(2,1)S(1)} custom-call(bf16[1040,576]{1,0:T(8,128)(2,1)S(1)} %copy-done.11, bf16[16,72,576]{2,1,0:T(8,128)(2,1)S(1)} %all-to-all-done.1.message_ref, bf16[1040,576]{1,0:T(8,128)(2,1)S(1)} %copy-done.6, f32[1,512]{1,0:T(1,128)S(1)} %select_n.77.seen_ref, bf16[512,128]{1,0:T(8,128)(2,1)S(1)} %copy-done.3), custom_call_target="tpu_custom_call" | custom-call | flops 3623878656 | bytes 4194304 | tf_op jit(solution)/shard_map/pallas_call | solution.py:322
  97.0 0.1 convolution_convert_fusion.3
  97.2 0.9 broadcast_in_dim.136
  98.1 7.4 %all-to-all-start.3 = ((bf16[32,65,128]{2,1,0:T(8,128)(2,1)}), bf16[32,65,128]{2,1,0:T(8,128)(2,1)S(1)}, u32[]{:S(2)}, u32[]{:S(2)}) async-start(bf16[32,65,128]{2,1,0:T(8,128)(2,1)} %bitcast.15), calls=%async_computation.3 | async-start | bytes 1179648 | tf_op jit(solution)/shard_map/all_to_all | solution.py:490
  105.7 10.9 %all-to-all-done.3 = bf16[32,65,128]{2,1,0:T(8,128)(2,1)S(1)} async-done(((bf16[32,65,128]{2,1,0:T(8,128)(2,1)}), bf16[32,65,128]{2,1,0:T(8,128)(2,1)S(1)}, u32[]{:S(2)}, u32[]{:S(2)}) %all-to-all-start.3) | async-done | bytes 532512 | tf_op jit(solution)/shard_map/all_to_all | solution.py:490
  116.7 0.1 pad.19
  116.8 0.1 copy.80
  117.0 2.9 fusion.33
  120.0 0.1 collective-permute-start
  120.1 0.2 select_reduce_fusion
  120.4 0.1 copy.77
  120.5 0.7 add.167.table
  121.2 0.4 collective-permute-done
  121.7 1.2 fusion.6
  123.0 0.1 fusion.8
  123.2 0.7 slice.44.rows_ref
  123.9 3.5 %shard_map.211 = bf16[64,2,10,16,128]{4,3,2,1,0:T(8,128)(2,1)} custom-call(s32[640]{0:T(1024)} %add.167.table, bf16[65,16,128]{2,1,0:T(8,128)(2,1)} %slice.44.rows_ref), custom_call_target="tpu_custom_call" | custom-call | tf_op jit(solution)/shard_map/pallas_call | solution.py:91
  127.4 70.3 %all_to_all.30 = bf16[128,160,128]{2,1,0:T(8,128)(2,1)} all-to-all(bf16[128,160,128]{2,1,0:T(8,128)(2,1)} %bitcast.66), channel_id=1, replica_groups=mesh['x'=4,'core'=2,'exp'=16] {'x','core','exp'}, dimensions={0} | all-to-all | bytes 10485760 | tf_op jit(solution)/shard_map/all_to_all | solution.py:520
  197.8 20.5 %shard_map.212 = bf16[1280,16,128]{2,1,0:T(8,128)(2,1)} custom-call(bf16[1280,16,128]{2,1,0:T(8,128)(2,1)} %bitcast.68, bf16[1,704,2048]{2,1,0:T(8,128)(2,1)} %bitcast.81, bf16[1,704,2048]{2,1,0:T(8,128)(2,1)} %bitcast.82, bf16[1,704,2048]{2,1,0:T(8,128)(2,1)} %down_hbm.1), custom_call_target="tpu_custom_call" | custom-call | flops 11072962560 | bytes 10485760 | tf_op jit(solution)/shard_map/pallas_call | solution.py:178
  218.3 7.9 %all-to-all-start.5 = ((bf16[128,160,128]{2,1,0:T(8,128)(2,1)}), bf16[128,160,128]{2,1,0:T(8,128)(2,1)}, u32[]{:S(2)}, u32[]{:S(2)}) async-start(bf16[128,160,128]{2,1,0:T(8,128)(2,1)} %bitcast.67), calls=%async_computation.5 | async-start | bytes 10485760 | tf_op jit(solution)/shard_map/all_to_all | solution.py:520
  226.2 0.1 copy.68
  226.3 0.1 reshape.207.slots
  226.4 0.2 fusion.2
  226.7 0.1 copy.76
  226.9 0.1 div.30.gates
  227.1 65.6 %all-to-all-done.5 = bf16[128,160,128]{2,1,0:T(8,128)(2,1)} async-done(((bf16[128,160,128]{2,1,0:T(8,128)(2,1)}), bf16[128,160,128]{2,1,0:T(8,128)(2,1)}, u32[]{:S(2)}, u32[]{:S(2)}) %all-to-all-start.5) | async-done | bytes 5242912 | tf_op jit(solution)/shard_map/all_to_all | solution.py:520
  292.6 6.1 %shard_map.213 = bf16[65,16,128]{2,1,0:T(8,128)(2,1)S(1)} custom-call(s32[390]{0:T(512)S(1)} %reshape.207.slots, f32[390]{0:T(512)S(1)} %div.30.gates, bf16[64,2,10,16,128]{4,3,2,1,0:T(8,128)(2,1)} %bitcast.24.half_ref, bf16[65,16,128]{2,1,0:T(8,128)(2,1)S(1)} %slice.45.resid_ref), custom_call_target="tpu_custom_call" | custom-call | tf_op jit(solution)/shard_map/pallas_call | solution.py:127
  298.8 0.8 copy.83
  (77 shorter events, 1.5 us)
Async XLA Ops:
  6.5 1.0 copy-start
  6.5 110.5 %all-gather.2.cloned.1.call-start = ((), (), s32[]{:S(2)}) async-start(), calls=%async_computation.6 | async-start | bytes 4456448 | tf_op jit(solution)/shard_map/all_gather | solution.py:396
  8.3 10.4 %copy-start.16 = (s32[16]{0:T(128)S(1)}, s32[16]{0:T(128)}, u32[]{:S(2)}) copy-start(s32[16]{0:T(128)} %param.42) | copy-start | bytes 196
  10.8 20.2 %copy-start.18 = (bf16[2048]{0:T(1024)(128)(2,1)S(1)}, bf16[2048]{0:T(1024)(128)(2,1)}, u32[]{:S(2)}) copy-start(bf16[2048]{0:T(1024)(128)(2,1)} %param.23) | copy-start | bytes 12292
  10.8 20.2 %copy-start.8 = (bf16[2048,64]{0,1:T(8,128)(2,1)S(1)}, bf16[2048,64]{0,1:T(8,128)(2,1)}, u32[]{:S(2)}) copy-start(bf16[2048,64]{0,1:T(8,128)(2,1)} %param.25) | copy-start | bytes 786436
  12.4 19.8 %copy-start.1 = (bf16[2048,128]{1,0:T(8,128)(2,1)S(1)}, bf16[2048,128]{1,0:T(8,128)(2,1)}, u32[]{:S(2)}) copy-start(bf16[2048,128]{1,0:T(8,128)(2,1)} %nope_ref.1) | copy-start | bytes 1572868
  12.4 19.8 %copy-start.2 = (bf16[512,128]{1,0:T(8,128)(2,1)S(1)}, bf16[512,128]{1,0:T(8,128)(2,1)}, u32[]{:S(2)}) copy-start(bf16[512,128]{1,0:T(8,128)(2,1)} %uk_ref.1) | copy-start | bytes 393220
  13.6 16.1 %all-to-all-start = ((bf16[8,64,576]{2,1,0:T(8,128)(2,1)}), bf16[8,64,576]{2,1,0:T(8,128)(2,1)S(1)}, u32[]{:S(2)}, u32[]{:S(2)}) async-start(bf16[8,64,576]{2,1,0:T(8,128)(2,1)} %bitcast.2), calls=%async_computation | async-start | bytes 1310720 | tf_op jit(solution)/shard_map/all_to_all | solution.py:428
  24.6 9.0 %copy-start.13 = (f32[1040,32]{1,0:T(8,128)}, f32[1040,32]{1,0:T(8,128)S(1)}, u32[]{:S(2)}) copy-start(f32[1040,32]{1,0:T(8,128)S(1)} %get-tuple-element.19) | copy-start | bytes 399364
  24.6 10.6 %copy-start.12 = (f32[1040,32]{1,0:T(8,128)}, f32[1040,32]{1,0:T(8,128)S(1)}, u32[]{:S(2)}) copy-start(f32[1040,32]{1,0:T(8,128)S(1)} %get-tuple-element.18) | copy-start | bytes 399364
  33.6 10.4 %copy-start.19 = (bf16[512]{0:T(512)(128)(2,1)S(1)}, bf16[512]{0:T(512)(128)(2,1)}, u32[]{:S(2)}) copy-start(bf16[512]{0:T(512)(128)(2,1)} %param.28) | copy-start | bytes 3076
  35.2 11.6 %copy-start.9 = (bf16[2048,64]{0,1:T(8,128)(2,1)S(1)}, bf16[2048,64]{0,1:T(8,128)(2,1)}, u32[]{:S(2)}) copy-start(bf16[2048,64]{0,1:T(8,128)(2,1)} %param.27) | copy-start | bytes 786436
  35.2 40.1 %all-to-all-start.1 = ((bf16[16,72,576]{2,1,0:T(8,128)(2,1)}), bf16[16,72,576]{2,1,0:T(8,128)(2,1)S(1)}, u32[]{:S(2)}, u32[]{:S(2)}) async-start(bf16[16,72,576]{2,1,0:T(8,128)(2,1)} %maximum_maximum_fusion), calls=%async_computation.1 | async-start | bytes 2949120 | tf_op jit(solution)/shard_map/all_to_all | solution.py:473
  46.8 2.2 copy-start.4
  49.0 1.7 copy-start.7
  50.6 36.3 %copy-start.3 = (bf16[512,128]{1,0:T(8,128)(2,1)S(1)}, bf16[512,128]{1,0:T(8,128)(2,1)}, u32[]{:S(2)}) copy-start(bf16[512,128]{1,0:T(8,128)(2,1)} %uv_ref.1) | copy-start | bytes 393220
  58.3 1.1 copy-start.10
  59.4 1.1 copy-start.5
  77.8 19.1 %all-to-all-start.2 = ((bf16[16,2,256]{2,1,0:T(2,128)(2,1)}), bf16[16,2,256]{2,1,0:T(2,128)(2,1)S(1)}, u32[]{:S(2)}, u32[]{:S(2)}) async-start(bf16[16,2,256]{2,1,0:T(2,128)(2,1)} %reshape.222), calls=%async_computation.2 | async-start | bytes 32768 | tf_op jit(solution)/shard_map/all_to_all | solution.py:480
  86.9 1.3 copy-start.6
  88.2 1.3 copy-start.11
  96.9 8.6 %copy-start.15 = (s32[65,6]{0,1:T(8,128)S(1)}, s32[65,6]{0,1:T(8,128)}, u32[]{:S(2)}) copy-start(s32[65,6]{0,1:T(8,128)} %param.37) | copy-start | bytes 4684
  98.1 18.5 %all-to-all-start.3 = ((bf16[32,65,128]{2,1,0:T(8,128)(2,1)}), bf16[32,65,128]{2,1,0:T(8,128)(2,1)S(1)}, u32[]{:S(2)}, u32[]{:S(2)}) async-start(bf16[32,65,128]{2,1,0:T(8,128)(2,1)} %bitcast.15), calls=%async_computation.3 | async-start | bytes 1179648 | tf_op jit(solution)/shard_map/all_to_all | solution.py:490
  117.0 3.4 %copy-start.17 = (bf16[2048]{0:T(1024)(128)(2,1)S(1)}, bf16[2048]{0:T(1024)(128)(2,1)}, u32[]{:S(2)}) copy-start(bf16[2048]{0:T(1024)(128)(2,1)} %param.32) | copy-start | bytes 12292
  120.0 1.7 collective-permute-start
  218.2 8.2 %copy-start.14 = (bf16[2048,64]{0,1:T(8,128)(2,1)S(1)}, bf16[2048,64]{0,1:T(8,128)(2,1)}, u32[]{:S(2)}) copy-start(bf16[2048,64]{0,1:T(8,128)(2,1)} %param.33) | copy-start | bytes 786436
  218.3 74.4 %all-to-all-start.5 = ((bf16[128,160,128]{2,1,0:T(8,128)(2,1)}), bf16[128,160,128]{2,1,0:T(8,128)(2,1)}, u32[]{:S(2)}, u32[]{:S(2)}) async-start(bf16[128,160,128]{2,1,0:T(8,128)(2,1)} %bitcast.67), calls=%async_computation.5 | async-start | bytes 10485760 | tf_op jit(solution)/shard_map/all_to_all | solution.py:520
Sparse Core Ops, SparseCore 0:
  9.5 70.7 all-gather.1

commit v3 on v2

--- a/solution.py
+++ b/solution.py
@@ -105,39 +105,53 @@
     )(table, rows)
 
 
-def combine_kernel(slots, gates, half_ref, resid_ref, out_ref):
-    cap = half_ref.shape[2]
-
+def combine_kernel(cap, slots, gates, half_ref, resid_ref, out_ref):
     def one(t, carry):
-        total = resid_ref[t].astype(F32)
-        mixed = jnp.zeros_like(total)
+        mixed = jnp.zeros(out_ref.shape[1:], F32)
         for k in range(TOP):
             slot = slots[t * TOP + k]
-            expert = slot // cap
-            place = slot - expert * cap
-            both = half_ref[expert, 0, place].astype(F32) + half_ref[expert, 1, place].astype(F32)
+            both = half_ref[slot].astype(F32) + half_ref[slot + cap].astype(F32)
             mixed = mixed + gates[t * TOP + k] * both.astype(BF16).astype(F32)
-        out_ref[t] = (total + mixed).astype(BF16)
+        out_ref[t] = (resid_ref[t].astype(F32) + mixed).astype(BF16)
         return carry
 
     lax.fori_loop(0, out_ref.shape[0], one, 0, unroll=5)
 
 
-def combine_rows(slots, gates, halves, resid):
-    return pl.pallas_call(
-        combine_kernel,
-        grid_spec=pltpu.PrefetchScalarGridSpec(
-            num_scalar_prefetch=2,
-            grid=(1,),
-            in_specs=[
-                pl.BlockSpec(halves.shape, lambda i, s, g: (0, 0, 0, 0, 0)),
-                pl.BlockSpec(resid.shape, lambda i, s, g: (0, 0, 0)),
-            ],
-            out_specs=pl.BlockSpec(resid.shape, lambda i, s, g: (0, 0, 0)),
-        ),
+def combine_rows(cap, slots, gates, halves, resid):
+    return pl.pallas_call(
+        functools.partial(combine_kernel, cap),
+        in_specs=[pl.BlockSpec(memory_space=pltpu.SMEM)] * 2
+        + [pl.BlockSpec(memory_space=pltpu.VMEM)] * 2,
+        out_specs=pl.BlockSpec(memory_space=pltpu.VMEM),
         out_shape=jax.ShapeDtypeStruct(resid.shape, BF16),
         compiler_params=pltpu.CompilerParams(vmem_limit_bytes=32 * MIB),
     )(slots, gates, halves, resid)
+
+
+def order_kernel(dest, latent_ref, rope_ref, out_ref, taken):
+    move = out_ref.shape[0] // taken.shape[0]
+    for g in range(taken.shape[0]):
+        taken[g] = 0
+    for i in range(out_ref.shape[0]):
+        group = dest[i]
+        place = group * move + taken[group]
+        taken[group] = taken[group] + 1
+        out_ref[place, :, :RANK] = latent_ref[i, 0]
+        out_ref[place, :, RANK:] = rope_ref[i]
+
+
+def order_pages(dest, latent, rope, groups):
+    slots, _, page, _ = latent.shape
+    return pl.pallas_call(
+        order_kernel,
+        in_specs=[pl.BlockSpec(memory_space=pltpu.SMEM)]
+        + [pl.BlockSpec(memory_space=pltpu.VMEM)] * 2,
+        out_specs=pl.BlockSpec(memory_space=pltpu.VMEM),
+        out_shape=jax.ShapeDtypeStruct((slots, page, KEY), BF16),
+        scratch_shapes=[pltpu.SMEM((groups,), jnp.int32)],
+        compiler_params=pltpu.CompilerParams(vmem_limit_bytes=32 * MIB),
+    )(dest, latent, rope)
 
 
 def expert_kernel(x_ref, gate_hbm, up_hbm, down_hbm, out_ref, gate_ref, up_ref, down_ref, sems):
@@ -158,8 +172,8 @@
 
     rows, blocks, lanes = x_ref.shape
     x = x_ref[...].reshape(rows, blocks * lanes)
-    hidden_gate = dot_t(x, gate_ref[0])
-    hidden_up = dot_t(x, up_ref[0])
+    hidden_gate = dot(x, gate_ref[0])
+    hidden_up = dot(x, up_ref[0])
     hidden = (hidden_gate / (1.0 + jnp.exp(-hidden_gate)) * hidden_up).astype(BF16)
 
     @pl.when(opening)
@@ -186,9 +200,9 @@
         + [pltpu.SemaphoreType.DMA((3,))],
         compiler_params=pltpu.CompilerParams(vmem_limit_bytes=60 * MIB),
         cost_estimate=pl.CostEstimate(
-            flops=6 * rows * blocks * lanes * weights[0].shape[1],
+            flops=6 * rows * blocks * lanes * weights[0].shape[2],
             bytes_accessed=4 * rows * blocks * lanes,
-            transcendentals=rows * weights[0].shape[1],
+            transcendentals=rows * weights[0].shape[2],
         ),
     )(x, *weights)
 
@@ -409,7 +423,8 @@
     before = (row_ids[None, :] < row_ids[:, None]).astype(BF16)
     rank = dot(before, member.astype(BF16)).astype(jnp.int32)
     slot_of = jnp.sum(
-        jnp.where(named, rank[:, None, :] + expert_ids[None, None, :] * capacity, 0), axis=2
+        jnp.where(named, rank[:, None, :] + expert_ids[None, None, :] * (2 * capacity), 0),
+        axis=2,
     )
     place_ids = jnp.arange(capacity, dtype=jnp.int32)
     filled = member[:, :, None] & (rank[:, :, None] == place_ids[None, None, :])
@@ -417,14 +432,9 @@
         jnp.where(filled, row_ids[:, None, None] - rows_device, 0), axis=0
     )
 
-    slot_ids = jnp.arange(req_group, dtype=jnp.int32)
-    earlier = (mig_dest[None, :] == mig_dest[:, None]) & (slot_ids[None, :] < slot_ids[:, None])
-    placed = mig_dest * move_count + jnp.sum(earlier.astype(jnp.int32), axis=1)
-    order = (placed[None, :] == slot_ids[:, None]).astype(BF16)
-    pages = jnp.concatenate(
-        [cache_latent[:, 0], cache_rope.reshape(req_group, page_size, DR)], axis=2
-    )
-    outgoing = jnp.einsum("os,sik->oik", order, pages, preferred_element_type=F32).astype(BF16)
+    outgoing = order_pages(
+        mig_dest, cache_latent, cache_rope.reshape(req_group, page_size, DR), req_count
+    )
     arrived = lax.all_to_all(
         outgoing.reshape(req_count, move_count * page_size, KEY),
         REQ,
@@ -434,10 +444,8 @@
     ).reshape(req_group, page_size, KEY)
 
     span_len = lax.dynamic_index_in_dim(cache_len, span_slot[0], 0, keepdims=False)
-    positions = jnp.concatenate([span_len + jnp.arange(SPAN, dtype=jnp.int32), cache_len])
-    angles = rope_angles(positions, DR)
-    cosine, sine = jnp.cos(angles), jnp.sin(angles)
-    late_cosine, late_sine = cosine[SPAN:], sine[SPAN:]
+    late_angles = rope_angles(cache_len, DR)
+    late_cosine, late_sine = jnp.cos(late_angles), jnp.sin(late_angles)
     late = rms_scale(tokens[SPAN:], attn_gain).astype(BF16)
     late_query = jnp.concatenate(
         [
@@ -457,9 +465,12 @@
         ],
         axis=1,
     )
+    positions = jnp.concatenate([span_len + jnp.arange(SPAN, dtype=jnp.int32), cache_len])
+    angles = rope_angles(positions, DR) + after(message)
+    cosine, sine = jnp.cos(angles), jnp.sin(angles)
     query, new_keys = project(
         tokens,
-        (attn_gain + after(message).astype(BF16))[None, :],
+        attn_gain[None, :],
         wq_nope,
         wq_rope.T,
         w_krope.T,
@@ -535,12 +546,13 @@
     )
     computed = expert_rows(
         received.reshape(device_count * capacity, blocks, LANES),
-        (jnp.swapaxes(w_gate, 1, 2), jnp.swapaxes(w_up, 1, 2), w_down),
+        (w_gate, w_up, w_down),
     )
     mixed = combine_rows(
+        capacity,
         slot_of.reshape(-1),
         gate_w.reshape(-1),
-        spread(computed).reshape(expert_count, 2, capacity, blocks, LANES),
+        spread(computed).reshape(device_count * capacity, blocks, LANES),
         resid.reshape(rows_device, blocks, LANES),
     )
     return mixed.reshape(rows_device, width)

time: 308 us -> 297 us (0.964)
  blocking collectives: 70.3 us -> 0 us
  waiting for transfers between devices: 96.9 us -> 152 us
  local copies, waits for them, and re-layouts: 21.6 us -> 27.7 us
  other arithmetic: 13.6 us -> 9.86 us
  starting transfers between devices: 36.9 us -> 40.6 us
    all_to_all x1 -> x0, blocking collectives: 70.3 us -> none  [spread(): lax.all_to_all(rows.reshape(device_count, capacity * blocks, LANES), FLAT...]
    all_to_all x1 -> x2, waiting for transfers between devices: 65.6 us -> 124 us  [spread(): lax.all_to_all(rows.reshape(device_count, capacity * blocks, LANES), FLAT...]
    unnamed x49 -> x58, local copies, waits for them, and re-layouts: 12.9 us -> 20 us
    all_to_all x1 -> x2, starting transfers between devices: 7.85 us -> 11.7 us  [spread(): lax.all_to_all(rows.reshape(device_count, capacity * blocks, LANES), FLAT...]
  transfers between devices with their start and end apart: 7 -> 8, of which waited for: 5 -> 6; matrix products, arithmetic and copies ran while one was open for 8% -> 9% of each run, Pallas kernels for 5% -> 6%
where the time goes in v3:
time: 297 us; the launch traced here: 296 us
  waiting for transfers between devices  152 us (51%)
  Pallas kernels  44.3 us (15%)
  starting transfers between devices  40.6 us (14%)
  local copies, waits for them, and re-layouts  27.7 us (9%)
  between operations  15.4 us (5%)
  other arithmetic  9.86 us (3%)
  matrix products  5.66 us (2%)
    all_to_all x2, waiting for transfers between devices, spread(): lax.all_to_all(rows.reshape(device_count, capacity * blocks, LANES), FLAT...  124 us
    pallas_call x1, Pallas kernels, expert_rows(): pl.pallas_call(expert_kernel, grid=(rows // step,), in_specs=[pl.BlockSpe...  20.4 us
    unnamed x58, local copies, waits for them, and re-layouts  20 us
    all_to_all x1, waiting for transfers between devices, shards(): lax.all_to_all(message, 'exp', split_axis=0, concat_axis=0, tiled=True)  12.9 us
    all_to_all x2, starting transfers between devices, spread(): lax.all_to_all(rows.reshape(device_count, capacity * blocks, LANES), FLAT...  11.7 us
    all_to_all x1, waiting for transfers between devices, shards(): lax.all_to_all(jnp.broadcast_to(head_out.reshape(1, exp_count, rows_devic...  10.9 us
    all_to_all x1, starting transfers between devices, shards(): lax.all_to_all(own_out[:, None, :], 'exp', split_axis=0, concat_axis=0, t...  8.88 us
    all_to_all x1, starting transfers between devices, shards(): lax.all_to_all(message, 'exp', split_axis=0, concat_axis=0, tiled=True)  8.2 us
  transfers between devices with their start and end apart: 8, of which 6 were waited for; matrix products, arithmetic and copies ran while one was open for 9% of the time, Pallas kernels for 6%

profile of v3, /device:TPU:32, one launch (start us, length us, event | category | flops | bytes accessed | tf_op | source)
XLA Modules:
  0.0 295.5 jit_solution(15057465677346723775)
XLA Ops:
  6.6 1.0 copy-done
  7.6 0.7 constant_dynamic-slice_fusion
  8.3 1.0 reshape.205.rope_ref
  9.4 1.0 copy-done.2
  10.4 0.7 copy-done.7
  11.1 1.5 shard_map.208
  12.5 4.3 %all-to-all-start = ((bf16[8,64,576]{2,1,0:T(8,128)(2,1)}), bf16[8,64,576]{2,1,0:T(8,128)(2,1)S(1)}, u32[]{:S(2)}, u32[]{:S(2)}) async-start(bf16[8,64,576]{2,1,0:T(8,128)(2,1)} %bitcast.4), calls=%async_computation | async-start | bytes 1310720 | tf_op jit(solution)/shard_map/all_to_all | solution.py:438
  17.5 1.0 fusion.12
  18.5 1.1 fusion.27
  19.6 0.1 fusion.22
  19.8 1.2 convolution_convert_fusion.1
  21.2 0.6 fusion.34
  21.8 0.8 fusion.31
  22.7 0.6 iota_add_fusion
  23.3 0.7 fusion.25
  24.0 0.7 fusion.26
  24.7 3.9 %all-to-all-done = bf16[8,64,576]{2,1,0:T(8,128)(2,1)S(1)} async-done(((bf16[8,64,576]{2,1,0:T(8,128)(2,1)}), bf16[8,64,576]{2,1,0:T(8,128)(2,1)S(1)}, u32[]{:S(2)}, u32[]{:S(2)}) %all-to-all-start) | async-done | bytes 589856 | tf_op jit(solution)/shard_map/all_to_all | solution.py:438
  28.7 1.6 maximum_maximum_fusion
  30.3 8.2 %all-to-all-start.1 = ((bf16[16,72,576]{2,1,0:T(8,128)(2,1)}), bf16[16,72,576]{2,1,0:T(8,128)(2,1)S(1)}, u32[]{:S(2)}, u32[]{:S(2)}) async-start(bf16[16,72,576]{2,1,0:T(8,128)(2,1)} %maximum_maximum_fusion), calls=%async_computation.1 | async-start | bytes 2949120 | tf_op jit(solution)/shard_map/all_to_all | solution.py:484
  38.7 0.5 slice.29
  39.9 2.0 fusion.11
  41.9 0.3 pad_maximum_fusion
  42.3 2.4 copy-done.6
  44.7 7.5 %shard_map.209 = (bf16[1040,576]{1,0:T(8,128)(2,1)S(1)}, bf16[1040,576]{1,0:T(8,128)(2,1)S(1)}) custom-call(bf16[1040,2048]{1,0:T(8,128)(2,1)S(1)} %copy-done.6, bf16[1,2048]{1,0:T(2,128)(2,1)S(1)} %broadcast_in_dim.125.gain_ref, bf16[2048,128]{1,0:T(8,128)(2,1)S(1)} %copy-done.3, bf16[64,2048]{1,0:T(8,128)(2,1)S(1)} %bitcast.56, ...), custom_call_target="tpu_custom_call" | custom-call | flops 3271557120 | bytes 9801728 | tf_op jit(solution)/shard_map/pallas_call | solution.py:251
  52.2 1.1 copy-done.13
  53.4 1.1 copy-done.8
  54.5 12.9 %all-to-all-done.1.message_ref = bf16[16,72,576]{2,1,0:T(8,128)(2,1)S(1)} async-done(((bf16[16,72,576]{2,1,0:T(8,128)(2,1)}), bf16[16,72,576]{2,1,0:T(8,128)(2,1)S(1)}, u32[]{:S(2)}, u32[]{:S(2)}) %all-to-all-start.1) | async-done | bytes 1327136 | tf_op jit(solution)/shard_map/all_to_all | solution.py:484
  67.4 0.6 shard_map.211
  68.0 0.6 broadcast.171
  68.6 0.7 reduce.1
  69.3 0.6 reshape.218
  69.9 8.9 %all-to-all-start.2 = ((bf16[16,2,256]{2,1,0:T(2,128)(2,1)}), bf16[16,2,256]{2,1,0:T(2,128)(2,1)S(1)}, u32[]{:S(2)}, u32[]{:S(2)}) async-start(bf16[16,2,256]{2,1,0:T(2,128)(2,1)} %reshape.218), calls=%async_computation.2 | async-start | bytes 32768 | tf_op jit(solution)/shard_map/all_to_all | solution.py:491
  78.8 1.3 copy-done.9
  80.1 1.3 copy-done.14
  81.4 7.4 %shard_map.210 = bf16[1024,128]{1,0:T(8,128)(2,1)S(1)} custom-call(bf16[1040,576]{1,0:T(8,128)(2,1)S(1)} %copy-done.14, bf16[16,72,576]{2,1,0:T(8,128)(2,1)S(1)} %all-to-all-done.1.message_ref, bf16[1040,576]{1,0:T(8,128)(2,1)S(1)} %copy-done.9, f32[1,512]{1,0:T(1,128)S(1)} %select_n.77.seen_ref, bf16[512,128]{1,0:T(8,128)(2,1)S(1)} %copy-done.5), custom_call_target="tpu_custom_call" | custom-call | flops 3623878656 | bytes 4194304 | tf_op jit(solution)/shard_map/pallas_call | solution.py:336
  88.8 0.1 convolution_convert_fusion.2
  89.1 0.9 broadcast_in_dim.138
  90.0 7.4 %all-to-all-start.3 = ((bf16[32,65,128]{2,1,0:T(8,128)(2,1)}), bf16[32,65,128]{2,1,0:T(8,128)(2,1)S(1)}, u32[]{:S(2)}, u32[]{:S(2)}) async-start(bf16[32,65,128]{2,1,0:T(8,128)(2,1)} %bitcast.13), calls=%async_computation.3 | async-start | bytes 1179648 | tf_op jit(solution)/shard_map/all_to_all | solution.py:501
  97.5 10.9 %all-to-all-done.3 = bf16[32,65,128]{2,1,0:T(8,128)(2,1)S(1)} async-done(((bf16[32,65,128]{2,1,0:T(8,128)(2,1)}), bf16[32,65,128]{2,1,0:T(8,128)(2,1)S(1)}, u32[]{:S(2)}, u32[]{:S(2)}) %all-to-all-start.3) | async-done | bytes 532512 | tf_op jit(solution)/shard_map/all_to_all | solution.py:501
  108.6 0.1 copy.86
  108.8 2.9 fusion.35
  111.8 0.1 collective-permute-start
  111.9 0.2 select_reduce_fusion
  112.3 0.7 add.163.table
  113.0 0.4 collective-permute-done
  113.5 1.2 fusion.3
  114.8 0.1 fusion.5
  114.9 0.7 copy-done.16
  115.7 0.7 slice.34.rows_ref
  116.4 3.5 %shard_map.212 = bf16[64,2,10,16,128]{4,3,2,1,0:T(8,128)(2,1)} custom-call(s32[640]{0:T(1024)} %add.163.table, bf16[65,16,128]{2,1,0:T(8,128)(2,1)} %slice.34.rows_ref), custom_call_target="tpu_custom_call" | custom-call | tf_op jit(solution)/shard_map/pallas_call | solution.py:91
  120.0 6.8 %all-to-all-start.4 = ((bf16[128,160,128]{2,1,0:T(8,128)(2,1)}), bf16[128,160,128]{2,1,0:T(8,128)(2,1)}, u32[]{:S(2)}, u32[]{:S(2)}) async-start(bf16[128,160,128]{2,1,0:T(8,128)(2,1)} %bitcast.58), calls=%async_computation.4 | async-start | bytes 10485760 | tf_op jit(solution)/shard_map/all_to_all | solution.py:531
  126.8 2.9 copy.82.gate_hbm
  129.7 4.6 %copy.83.up_hbm = bf16[1,2048,704]{2,1,0:T(8,128)(2,1)} copy(bf16[1,2048,704]{1,2,0:T(8,128)(2,1)} %param.35) | data formatting | bytes 5767168 | tf_op args[13]
  134.3 58.7 %all-to-all-done.4 = bf16[128,160,128]{2,1,0:T(8,128)(2,1)} async-done(((bf16[128,160,128]{2,1,0:T(8,128)(2,1)}), bf16[128,160,128]{2,1,0:T(8,128)(2,1)}, u32[]{:S(2)}, u32[]{:S(2)}) %all-to-all-start.4) | async-done | bytes 5242912 | tf_op jit(solution)/shard_map/all_to_all | solution.py:531
  193.0 20.4 %shard_map.213 = bf16[1280,16,128]{2,1,0:T(8,128)(2,1)} custom-call(bf16[1280,16,128]{2,1,0:T(8,128)(2,1)} %bitcast.18.x_ref, bf16[1,2048,704]{2,1,0:T(8,128)(2,1)} %copy.82.gate_hbm, bf16[1,2048,704]{2,1,0:T(8,128)(2,1)} %copy.83.up_hbm, bf16[1,704,2048]{2,1,0:T(8,128)(2,1)} %down_hbm.1), custom_call_target="tpu_custom_call" | custom-call | flops 11072962560 | bytes 10485760 | tf_op jit(solution)/shard_map/pallas_call | solution.py:192
  213.5 4.9 %all-to-all-start.5 = ((bf16[128,160,128]{2,1,0:T(8,128)(2,1)}), bf16[128,160,128]{2,1,0:T(8,128)(2,1)}, u32[]{:S(2)}, u32[]{:S(2)}) async-start(bf16[128,160,128]{2,1,0:T(8,128)(2,1)} %bitcast.59), calls=%async_computation.5 | async-start | bytes 10485760 | tf_op jit(solution)/shard_map/all_to_all | solution.py:531
  218.4 0.1 copy.74
  218.5 0.1 reshape.204.slots
  218.7 0.2 fusion.2
  219.0 0.1 copy.80
  219.1 0.1 div.30.gates
  219.3 65.1 %all-to-all-done.5 = bf16[128,160,128]{2,1,0:T(8,128)(2,1)} async-done(((bf16[128,160,128]{2,1,0:T(8,128)(2,1)}), bf16[128,160,128]{2,1,0:T(8,128)(2,1)}, u32[]{:S(2)}, u32[]{:S(2)}) %all-to-all-start.5) | async-done | bytes 5242912 | tf_op jit(solution)/shard_map/all_to_all | solution.py:531
  284.4 3.4 %shard_map.214 = bf16[65,16,128]{2,1,0:T(8,128)(2,1)S(1)} custom-call(s32[390]{0:T(512)S(1)} %reshape.204.slots, f32[390]{0:T(512)S(1)} %div.30.gates, bf16[1280,16,128]{2,1,0:T(8,128)(2,1)} %bitcast.20.half_ref, bf16[65,16,128]{2,1,0:T(8,128)(2,1)S(1)} %slice.35.resid_ref), custom_call_target="tpu_custom_call" | custom-call | tf_op jit(solution)/shard_map/pallas_call | solution.py:122
  287.9 0.8 copy.89
  (84 shorter events, 1.6 us)
Async XLA Ops:
  6.5 1.0 copy-start
  6.5 10.9 %copy-start.21 = (s32[16]{0:T(128)S(1)}, s32[16]{0:T(128)}, u32[]{:S(2)}) copy-start(s32[16]{0:T(128)} %param.42) | copy-start | bytes 196
  6.5 11.0 %copy-start.20 = (bf16[2048]{0:T(1024)(128)(2,1)S(1)}, bf16[2048]{0:T(1024)(128)(2,1)}, u32[]{:S(2)}) copy-start(bf16[2048]{0:T(1024)(128)(2,1)} %param.23) | copy-start | bytes 12292
  6.5 12.0 %copy-start.11 = (bf16[2048,64]{0,1:T(8,128)(2,1)S(1)}, bf16[2048,64]{0,1:T(8,128)(2,1)}, u32[]{:S(2)}) copy-start(bf16[2048,64]{0,1:T(8,128)(2,1)} %param.25) | copy-start | bytes 786436
  6.5 13.2 %copy-start.4 = (bf16[512,128]{1,0:T(8,128)(2,1)S(1)}, bf16[512,128]{1,0:T(8,128)(2,1)}, u32[]{:S(2)}) copy-start(bf16[512,128]{1,0:T(8,128)(2,1)} %uk_ref.1) | copy-start | bytes 393220
  6.5 13.2 %copy-start.3 = (bf16[2048,128]{1,0:T(8,128)(2,1)S(1)}, bf16[2048,128]{1,0:T(8,128)(2,1)}, u32[]{:S(2)}) copy-start(bf16[2048,128]{1,0:T(8,128)(2,1)} %nope_ref.1) | copy-start | bytes 1572868
  6.6 102.2 %all-gather.2.cloned.1.call-start = ((), (), s32[]{:S(2)}) async-start(), calls=%async_computation.6 | async-start | bytes 4456448 | tf_op jit(solution)/shard_map/all_gather | solution.py:410
  9.4 1.0 copy-start.2
  10.4 0.7 copy-start.7
  12.5 16.1 %all-to-all-start = ((bf16[8,64,576]{2,1,0:T(8,128)(2,1)}), bf16[8,64,576]{2,1,0:T(8,128)(2,1)S(1)}, u32[]{:S(2)}, u32[]{:S(2)}) async-start(bf16[8,64,576]{2,1,0:T(8,128)(2,1)} %bitcast.4), calls=%async_computation | async-start | bytes 1310720 | tf_op jit(solution)/shard_map/all_to_all | solution.py:438
  28.6 9.9 %copy-start.23 = (bf16[512]{0:T(512)(128)(2,1)S(1)}, bf16[512]{0:T(512)(128)(2,1)}, u32[]{:S(2)}) copy-start(bf16[512]{0:T(512)(128)(2,1)} %param.28) | copy-start | bytes 3076
  30.3 12.0 %copy-start.12 = (bf16[2048,64]{0,1:T(8,128)(2,1)S(1)}, bf16[2048,64]{0,1:T(8,128)(2,1)}, u32[]{:S(2)}) copy-start(bf16[2048,64]{0,1:T(8,128)(2,1)} %param.27) | copy-start | bytes 786436
  30.3 37.1 %all-to-all-start.1 = ((bf16[16,72,576]{2,1,0:T(8,128)(2,1)}), bf16[16,72,576]{2,1,0:T(8,128)(2,1)S(1)}, u32[]{:S(2)}, u32[]{:S(2)}) async-start(bf16[16,72,576]{2,1,0:T(8,128)(2,1)} %maximum_maximum_fusion), calls=%async_computation.1 | async-start | bytes 2949120 | tf_op jit(solution)/shard_map/all_to_all | solution.py:484
  38.7 3.6 %copy-start.10 = (bf16[2048,512]{1,0:T(8,128)(2,1)S(1)}, bf16[2048,512]{1,0:T(8,128)(2,1)}, u32[]{:S(2)}) copy-start(bf16[2048,512]{1,0:T(8,128)(2,1)} %latent_ref.3) | copy-start | bytes 6291460
  42.3 2.4 copy-start.6
  44.7 34.0 %copy-start.5 = (bf16[512,128]{1,0:T(8,128)(2,1)S(1)}, bf16[512,128]{1,0:T(8,128)(2,1)}, u32[]{:S(2)}) copy-start(bf16[512,128]{1,0:T(8,128)(2,1)} %uv_ref.1) | copy-start | bytes 393220
  52.2 1.1 copy-start.13
  53.4 1.1 copy-start.8
  69.9 18.9 %all-to-all-start.2 = ((bf16[16,2,256]{2,1,0:T(2,128)(2,1)}), bf16[16,2,256]{2,1,0:T(2,128)(2,1)S(1)}, u32[]{:S(2)}, u32[]{:S(2)}) async-start(bf16[16,2,256]{2,1,0:T(2,128)(2,1)} %reshape.218), calls=%async_computation.2 | async-start | bytes 32768 | tf_op jit(solution)/shard_map/all_to_all | solution.py:491
  78.7 1.3 copy-start.9
  80.1 1.3 copy-start.14
  88.8 8.6 %copy-start.19 = (s32[65,6]{0,1:T(8,128)S(1)}, s32[65,6]{0,1:T(8,128)}, u32[]{:S(2)}) copy-start(s32[65,6]{0,1:T(8,128)} %param.37) | copy-start | bytes 4684
  90.0 18.5 %all-to-all-start.3 = ((bf16[32,65,128]{2,1,0:T(8,128)(2,1)}), bf16[32,65,128]{2,1,0:T(8,128)(2,1)S(1)}, u32[]{:S(2)}, u32[]{:S(2)}) async-start(bf16[32,65,128]{2,1,0:T(8,128)(2,1)} %bitcast.13), calls=%async_computation.3 | async-start | bytes 1179648 | tf_op jit(solution)/shard_map/all_to_all | solution.py:501
  108.8 3.4 %copy-start.22 = (bf16[2048]{0:T(1024)(128)(2,1)S(1)}, bf16[2048]{0:T(1024)(128)(2,1)}, u32[]{:S(2)}) copy-start(bf16[2048]{0:T(1024)(128)(2,1)} %param.32) | copy-start | bytes 12292
  111.8 1.7 collective-permute-start
  114.9 0.7 copy-start.16
  120.0 6.9 %copy-start.15 = (bf16[1,2048,704]{1,2,0:T(8,128)(2,1)S(1)}, bf16[1,2048,704]{1,2,0:T(8,128)(2,1)}, u32[]{:S(2)}) copy-start(bf16[1,2048,704]{1,2,0:T(8,128)(2,1)} %param.34) | copy-start | bytes 8650756
  120.0 73.0 %all-to-all-start.4 = ((bf16[128,160,128]{2,1,0:T(8,128)(2,1)}), bf16[128,160,128]{2,1,0:T(8,128)(2,1)}, u32[]{:S(2)}, u32[]{:S(2)}) async-start(bf16[128,160,128]{2,1,0:T(8,128)(2,1)} %bitcast.58), calls=%async_computation.4 | async-start | bytes 10485760 | tf_op jit(solution)/shard_map/all_to_all | solution.py:531
  213.5 5.2 %copy-start.17 = (bf16[65,2048]{1,0:T(8,128)(2,1)S(1)}, bf16[65,2048]{1,0:T(8,128)(2,1)}, u32[]{:S(2)}) copy-start(bf16[65,2048]{1,0:T(8,128)(2,1)} %copy-done.16) | copy-start | bytes 798724
  213.5 5.2 %copy-start.18 = (bf16[2048,64]{0,1:T(8,128)(2,1)S(1)}, bf16[2048,64]{0,1:T(8,128)(2,1)}, u32[]{:S(2)}) copy-start(bf16[2048,64]{0,1:T(8,128)(2,1)} %param.33) | copy-start | bytes 786436
  213.5 70.9 %all-to-all-start.5 = ((bf16[128,160,128]{2,1,0:T(8,128)(2,1)}), bf16[128,160,128]{2,1,0:T(8,128)(2,1)}, u32[]{:S(2)}, u32[]{:S(2)}) async-start(bf16[128,160,128]{2,1,0:T(8,128)(2,1)} %bitcast.59), calls=%async_computation.5 | async-start | bytes 10485760 | tf_op jit(solution)/shard_map/all_to_all | solution.py:531
  284.4 4.3 %copy-start.1 = (bf16[128,2048]{1,0:T(8,128)(2,1)S(1)}, bf16[128,2048]{1,0:T(8,128)(2,1)}, u32[]{:S(2)}) copy-start(bf16[128,2048]{1,0:T(8,128)(2,1)} %param.31) | copy-start | bytes 1572868
Sparse Core Ops, SparseCore 0:
  9.5 65.0 all-gather.1

commit v4 on v3

--- a/solution.py
+++ b/solution.py
@@ -154,32 +154,12 @@
     )(dest, latent, rope)
 
 
-def expert_kernel(x_ref, gate_hbm, up_hbm, down_hbm, out_ref, gate_ref, up_ref, down_ref, sems):
-    copies = [
-        pltpu.make_async_copy(source, target, sems.at[i])
-        for i, (source, target) in enumerate(
-            ((gate_hbm, gate_ref), (up_hbm, up_ref), (down_hbm, down_ref))
-        )
-    ]
-    opening = pl.program_id(0) == 0
-
-    @pl.when(opening)
-    def _():
-        for copy in copies:
-            copy.start()
-        copies[0].wait()
-        copies[1].wait()
-
+def expert_kernel(x_ref, gate_ref, up_ref, down_ref, out_ref):
     rows, blocks, lanes = x_ref.shape
     x = x_ref[...].reshape(rows, blocks * lanes)
-    hidden_gate = dot(x, gate_ref[0])
-    hidden_up = dot(x, up_ref[0])
+    hidden_gate = dot_t(x, gate_ref[0])
+    hidden_up = dot_t(x, up_ref[0])
     hidden = (hidden_gate / (1.0 + jnp.exp(-hidden_gate)) * hidden_up).astype(BF16)
-
-    @pl.when(opening)
-    def _():
-        copies[2].wait()
-
     step = 4
     for n in range(0, blocks, step):
         part = dot(hidden, down_ref[0, :, n * lanes : (n + step) * lanes]).astype(BF16)
@@ -193,16 +173,14 @@
         expert_kernel,
         grid=(rows // step,),
         in_specs=[pl.BlockSpec((step, blocks, lanes), lambda i: (i, 0, 0))]
-        + [pl.BlockSpec(memory_space=pl.ANY)] * 3,
+        + [pl.BlockSpec(memory_space=pltpu.VMEM)] * 3,
         out_specs=pl.BlockSpec((step, blocks, lanes), lambda i: (i, 0, 0)),
         out_shape=jax.ShapeDtypeStruct((rows, blocks, lanes), BF16),
-        scratch_shapes=[pltpu.VMEM(w.shape, w.dtype) for w in weights]
-        + [pltpu.SemaphoreType.DMA((3,))],
-        compiler_params=pltpu.CompilerParams(vmem_limit_bytes=60 * MIB),
+        compiler_params=pltpu.CompilerParams(vmem_limit_bytes=52 * MIB),
         cost_estimate=pl.CostEstimate(
-            flops=6 * rows * blocks * lanes * weights[0].shape[2],
+            flops=6 * rows * blocks * lanes * weights[0].shape[1],
             bytes_accessed=4 * rows * blocks * lanes,
-            transcendentals=rows * weights[0].shape[2],
+            transcendentals=rows * weights[0].shape[1],
         ),
     )(x, *weights)
 
@@ -280,17 +258,17 @@
     raised = jnp.exp(scores - top)
     self_raised = jnp.exp(self_score - top)
     total = jnp.sum(raised, axis=1, keepdims=True) + self_raised
-    out_ref[...] = (
-        dot((raised / total).astype(BF16), cache[:, :RANK])
-        + (self_raised / total).astype(BF16).astype(F32) * own[:, :RANK]
-    ).astype(BF16)
+    attended = dot((raised / total).astype(BF16), cache[:, :RANK]) + (
+        self_raised / total
+    ).astype(BF16).astype(F32) * own[:, :RANK]
+    out_ref[...] = attended.astype(BF16).reshape(out_ref.shape)
 
 
 def decode(message, own_key, seen, scale):
     heads = message.shape[0]
     return pl.pallas_call(
         functools.partial(decode_kernel, scale),
-        out_shape=jax.ShapeDtypeStruct((heads, RANK), BF16),
+        out_shape=jax.ShapeDtypeStruct((heads, RANK // LANES, LANES), BF16),
         compiler_params=pltpu.CompilerParams(vmem_limit_bytes=16 * MIB),
         cost_estimate=pl.CostEstimate(
             flops=1 << 25, bytes_accessed=1 << 21, transcendentals=1 << 13
@@ -489,8 +467,8 @@
         message, own_key, seen_bias(own_pages, page_size, own_len), scale_factor
     )
     decode_out = lax.all_to_all(
-        own_out[:, None, :], "exp", split_axis=0, concat_axis=0, tiled=True
-    )[:, 0]
+        own_out, "exp", split_axis=0, concat_axis=0, tiled=True
+    ).reshape(req_group, RANK)
 
     span_table = lax.dynamic_index_in_dim(page_table, span_slot[0], 0, keepdims=False)
     span_out = attend(
@@ -536,6 +514,7 @@
             tiled=True,
         )
 
+    late_zero = after(moe_in).astype(BF16)
     received = spread(
         pack_rows(
             table.reshape(-1),
@@ -546,7 +525,7 @@
     )
     computed = expert_rows(
         received.reshape(device_count * capacity, blocks, LANES),
-        (w_gate, w_up, w_down),
+        tuple(w + late_zero for w in (jnp.swapaxes(w_gate, 1, 2), jnp.swapaxes(w_up, 1, 2), w_down)),
     )
     mixed = combine_rows(
         capacity,

time: 297 us -> 294 us (0.990)
  local copies, waits for them, and re-layouts: 27.7 us -> 22.5 us
  other arithmetic: 9.86 us -> 14.5 us
    unnamed x58, local copies, waits for them, and re-layouts: 20 us -> 14.1 us
    add x0 -> x3, other arithmetic: none -> 5.42 us  [shards(): w + late_zero]
  transfers between devices with their start and end apart: 8 -> 8, of which waited for: 6 -> 6; matrix products, arithmetic and copies ran while one was open for 9% -> 8% of each run, Pallas kernels for 6% -> 6%
where the time goes in v4:
time: 294 us; the launch traced here: 293 us
  waiting for transfers between devices  150 us (51%)
  Pallas kernels  44.1 us (15%)
  starting transfers between devices  40.5 us (14%)
  local copies, waits for them, and re-layouts  22.5 us (8%)
  between operations  16.1 us (5%)
  other arithmetic  14.5 us (5%)
  matrix products  5.66 us (2%)
    all_to_all x2, waiting for transfers between devices, spread(): lax.all_to_all(rows.reshape(device_count, capacity * blocks, LANES), FLAT...  122 us
    pallas_call x1, Pallas kernels, expert_rows(): pl.pallas_call(expert_kernel, grid=(rows // step,), in_specs=[pl.BlockSpe...  19.5 us
    unnamed x58, local copies, waits for them, and re-layouts  14.1 us
    all_to_all x1, waiting for transfers between devices, shards(): lax.all_to_all(message, 'exp', split_axis=0, concat_axis=0, tiled=True)  12.7 us
    all_to_all x2, starting transfers between devices, spread(): lax.all_to_all(rows.reshape(device_count, capacity * blocks, LANES), FLAT...  11.7 us
    all_to_all x1, waiting for transfers between devices, shards(): lax.all_to_all(jnp.broadcast_to(head_out.reshape(1, exp_count, rows_devic...  10.9 us
    all_to_all x1, starting transfers between devices, shards(): lax.all_to_all(own_out, 'exp', split_axis=0, concat_axis=0, tiled=True)  8.88 us
    all_to_all x1, starting transfers between devices, shards(): lax.all_to_all(message, 'exp', split_axis=0, concat_axis=0, tiled=True)  8.06 us
  transfers between devices with their start and end apart: 8, of which 6 were waited for; matrix products, arithmetic and copies ran while one was open for 8% of the time, Pallas kernels for 6%

profile of v4, /device:TPU:32, one launch (start us, length us, event | category | flops | bytes accessed | tf_op | source)
XLA Modules:
  0.0 293.1 jit_solution(735069708921340798)
XLA Ops:
  6.6 1.0 copy-done
  7.6 0.7 constant_dynamic-slice_fusion
  8.3 1.0 reshape.212.rope_ref
  9.4 1.0 copy-done.2
  10.4 0.7 copy-done.7
  11.1 1.5 shard_map.208
  12.5 4.3 %all-to-all-start = ((bf16[8,64,576]{2,1,0:T(8,128)(2,1)}), bf16[8,64,576]{2,1,0:T(8,128)(2,1)S(1)}, u32[]{:S(2)}, u32[]{:S(2)}) async-start(bf16[8,64,576]{2,1,0:T(8,128)(2,1)} %bitcast.4), calls=%async_computation | async-start | bytes 1310720 | tf_op jit(solution)/shard_map/all_to_all | solution.py:416
  17.6 1.0 fusion.12
  18.5 1.1 fusion.27
  19.6 0.1 fusion.22
  19.8 1.2 convolution_convert_fusion.1
  21.2 0.6 fusion.34
  21.8 0.7 fusion.31
  22.6 0.6 iota_add_fusion
  23.2 0.7 fusion.25
  23.9 0.6 fusion.26
  24.5 4.0 %all-to-all-done = bf16[8,64,576]{2,1,0:T(8,128)(2,1)S(1)} async-done(((bf16[8,64,576]{2,1,0:T(8,128)(2,1)}), bf16[8,64,576]{2,1,0:T(8,128)(2,1)S(1)}, u32[]{:S(2)}, u32[]{:S(2)}) %all-to-all-start) | async-done | bytes 589856 | tf_op jit(solution)/shard_map/all_to_all | solution.py:416
  28.7 1.6 maximum_maximum_fusion
  30.3 8.1 %all-to-all-start.1 = ((bf16[16,72,576]{2,1,0:T(8,128)(2,1)}), bf16[16,72,576]{2,1,0:T(8,128)(2,1)S(1)}, u32[]{:S(2)}, u32[]{:S(2)}) async-start(bf16[16,72,576]{2,1,0:T(8,128)(2,1)} %maximum_maximum_fusion), calls=%async_computation.1 | async-start | bytes 2949120 | tf_op jit(solution)/shard_map/all_to_all | solution.py:462
  38.6 0.5 slice.33
  39.9 2.0 fusion.11
  41.8 0.3 pad_maximum_fusion
  42.2 2.5 copy-done.6
  44.7 7.5 %shard_map.209 = (bf16[1040,576]{1,0:T(8,128)(2,1)S(1)}, bf16[1040,576]{1,0:T(8,128)(2,1)S(1)}) custom-call(bf16[1040,2048]{1,0:T(8,128)(2,1)S(1)} %copy-done.6, bf16[1,2048]{1,0:T(2,128)(2,1)S(1)} %broadcast_in_dim.122.gain_ref, bf16[2048,128]{1,0:T(8,128)(2,1)S(1)} %copy-done.3, bf16[64,2048]{1,0:T(8,128)(2,1)S(1)} %bitcast.60, ...), custom_call_target="tpu_custom_call" | custom-call | flops 3271557120 | bytes 9801728 | tf_op jit(solution)/shard_map/pallas_call | solution.py:229
  52.2 1.1 copy-done.13
  53.3 1.1 copy-done.8
  54.5 12.7 %all-to-all-done.1.message_ref = bf16[16,72,576]{2,1,0:T(8,128)(2,1)S(1)} async-done(((bf16[16,72,576]{2,1,0:T(8,128)(2,1)}), bf16[16,72,576]{2,1,0:T(8,128)(2,1)S(1)}, u32[]{:S(2)}, u32[]{:S(2)}) %all-to-all-start.1) | async-done | bytes 1327136 | tf_op jit(solution)/shard_map/all_to_all | solution.py:462
  67.1 1.2 shard_map.211
  68.4 8.9 %all-to-all-start.2 = ((bf16[16,4,128]{2,1,0:T(4,128)(2,1)}), bf16[16,4,128]{2,1,0:T(4,128)(2,1)S(1)}, u32[]{:S(2)}, u32[]{:S(2)}) async-start(bf16[16,4,128]{2,1,0:T(4,128)(2,1)} %shard_map.211), calls=%async_computation.2 | async-start | bytes 32768 | tf_op jit(solution)/shard_map/all_to_all | solution.py:469
  77.3 1.3 copy-done.9
  78.6 1.3 copy-done.14
  79.9 7.4 %shard_map.210 = bf16[1024,128]{1,0:T(8,128)(2,1)S(1)} custom-call(bf16[1040,576]{1,0:T(8,128)(2,1)S(1)} %copy-done.14, bf16[16,72,576]{2,1,0:T(8,128)(2,1)S(1)} %all-to-all-done.1.message_ref, bf16[1040,576]{1,0:T(8,128)(2,1)S(1)} %copy-done.9, f32[1,512]{1,0:T(1,128)S(1)} %select_n.77.seen_ref, bf16[512,128]{1,0:T(8,128)(2,1)S(1)} %copy-done.5), custom_call_target="tpu_custom_call" | custom-call | flops 3623878656 | bytes 4194304 | tf_op jit(solution)/shard_map/pallas_call | solution.py:314
  87.3 0.1 convolution_convert_fusion.2
  87.6 0.9 broadcast_in_dim.134
  88.5 7.4 %all-to-all-start.3 = ((bf16[32,65,128]{2,1,0:T(8,128)(2,1)}), bf16[32,65,128]{2,1,0:T(8,128)(2,1)S(1)}, u32[]{:S(2)}, u32[]{:S(2)}) async-start(bf16[32,65,128]{2,1,0:T(8,128)(2,1)} %bitcast.12), calls=%async_computation.3 | async-start | bytes 1179648 | tf_op jit(solution)/shard_map/all_to_all | solution.py:479
  96.0 10.9 %all-to-all-done.3 = bf16[32,65,128]{2,1,0:T(8,128)(2,1)S(1)} async-done(((bf16[32,65,128]{2,1,0:T(8,128)(2,1)}), bf16[32,65,128]{2,1,0:T(8,128)(2,1)S(1)}, u32[]{:S(2)}, u32[]{:S(2)}) %all-to-all-start.3) | async-done | bytes 532512 | tf_op jit(solution)/shard_map/all_to_all | solution.py:479
  107.1 0.1 copy.61
  107.3 2.9 %fusion.35 = f32[130,1024]{1,0:T(8,128)S(1)} fusion(bf16[130,2048]{1,0:T(8,128)(2,1)S(1)} %bitcast.70, bf16[2048,1024]{1,0:T(8,128)(2,1)} %all-gather.2.cloned.1.call-done), kind=kOutput, calls=%fused_computation.86 | convolution fusion | flops 545259520 | bytes 5259264 | tf_op jit(solution)/shard_map/dot_general | solution.py:50
  110.3 0.1 collective-permute-start
  110.5 0.2 select_reduce_fusion
  110.8 0.7 add.183.table
  111.6 0.4 collective-permute-done
  112.1 1.2 fusion.3
  113.3 0.1 fusion.5
  113.5 0.7 copy-done.18
  114.2 0.7 slice.39.rows_ref
  115.0 3.6 %shard_map.212 = bf16[64,2,10,16,128]{4,3,2,1,0:T(8,128)(2,1)} custom-call(s32[640]{0:T(1024)} %add.183.table, bf16[65,16,128]{2,1,0:T(8,128)(2,1)} %slice.39.rows_ref), custom_call_target="tpu_custom_call" | custom-call | tf_op jit(solution)/shard_map/pallas_call | solution.py:91
  118.5 6.8 %all-to-all-start.4 = ((bf16[128,160,128]{2,1,0:T(8,128)(2,1)}), bf16[128,160,128]{2,1,0:T(8,128)(2,1)}, u32[]{:S(2)}, u32[]{:S(2)}) async-start(bf16[128,160,128]{2,1,0:T(8,128)(2,1)} %bitcast.62), calls=%async_computation.4 | async-start | bytes 10485760 | tf_op jit(solution)/shard_map/all_to_all | solution.py:509
  125.4 1.3 slice.38
  127.4 1.8 add_bitcast_fusion.up_ref
  129.1 1.1 copy-done.16
  130.2 1.8 broadcast_add_fusion.down_ref
  132.0 1.1 copy-done.17
  133.1 1.9 add_bitcast_fusion.1.gate_ref
  134.9 56.6 %all-to-all-done.4 = bf16[128,160,128]{2,1,0:T(8,128)(2,1)} async-done(((bf16[128,160,128]{2,1,0:T(8,128)(2,1)}), bf16[128,160,128]{2,1,0:T(8,128)(2,1)}, u32[]{:S(2)}, u32[]{:S(2)}) %all-to-all-start.4) | async-done | bytes 5242912 | tf_op jit(solution)/shard_map/all_to_all | solution.py:509
  191.6 19.5 %shard_map.213 = bf16[1280,16,128]{2,1,0:T(8,128)(2,1)} custom-call(bf16[1280,16,128]{2,1,0:T(8,128)(2,1)} %bitcast.17.x_ref, bf16[1,704,2048]{2,1,0:T(8,128)(2,1)} %add_bitcast_fusion.1.gate_ref, bf16[1,704,2048]{2,1,0:T(8,128)(2,1)} %add_bitcast_fusion.up_ref, bf16[1,704,2048]{2,1,0:T(8,128)(2,1)} %broadcast_add_fusion.down_ref), custom_call_target="tpu_custom_call" | custom-call | flops 11072962560 | bytes 10485760 | tf_op jit(solution)/shard_map/pallas_call | solution.py:172
  211.1 4.9 %all-to-all-start.5 = ((bf16[128,160,128]{2,1,0:T(8,128)(2,1)}), bf16[128,160,128]{2,1,0:T(8,128)(2,1)}, u32[]{:S(2)}, u32[]{:S(2)}) async-start(bf16[128,160,128]{2,1,0:T(8,128)(2,1)} %bitcast.63), calls=%async_computation.5 | async-start | bytes 10485760 | tf_op jit(solution)/shard_map/all_to_all | solution.py:509
  216.1 0.1 reshape.211.slots
  216.3 0.2 fusion.2
  216.6 0.1 copy.57
  216.7 0.1 div.30.gates
  217.0 65.1 %all-to-all-done.5 = bf16[128,160,128]{2,1,0:T(8,128)(2,1)} async-done(((bf16[128,160,128]{2,1,0:T(8,128)(2,1)}), bf16[128,160,128]{2,1,0:T(8,128)(2,1)}, u32[]{:S(2)}, u32[]{:S(2)}) %all-to-all-start.5) | async-done | bytes 5242912 | tf_op jit(solution)/shard_map/all_to_all | solution.py:509
  282.0 3.4 %shard_map.214 = bf16[65,16,128]{2,1,0:T(8,128)(2,1)S(1)} custom-call(s32[390]{0:T(512)S(1)} %reshape.211.slots, f32[390]{0:T(512)S(1)} %div.30.gates, bf16[1280,16,128]{2,1,0:T(8,128)(2,1)} %bitcast.22.half_ref, bf16[65,16,128]{2,1,0:T(8,128)(2,1)S(1)} %slice.40.resid_ref), custom_call_target="tpu_custom_call" | custom-call | tf_op jit(solution)/shard_map/pallas_call | solution.py:122
  285.5 0.8 copy.64
  (86 shorter events, 1.7 us)
Async XLA Ops:
  6.5 1.0 copy-start
  6.5 11.0 %copy-start.23 = (s32[16]{0:T(128)S(1)}, s32[16]{0:T(128)}, u32[]{:S(2)}) copy-start(s32[16]{0:T(128)} %param.42) | copy-start | bytes 196
  6.5 11.0 %copy-start.22 = (bf16[2048]{0:T(1024)(128)(2,1)S(1)}, bf16[2048]{0:T(1024)(128)(2,1)}, u32[]{:S(2)}) copy-start(bf16[2048]{0:T(1024)(128)(2,1)} %param.23) | copy-start | bytes 12292
  6.5 12.0 %copy-start.11 = (bf16[2048,64]{0,1:T(8,128)(2,1)S(1)}, bf16[2048,64]{0,1:T(8,128)(2,1)}, u32[]{:S(2)}) copy-start(bf16[2048,64]{0,1:T(8,128)(2,1)} %param.25) | copy-start | bytes 786436
  6.5 13.2 %copy-start.4 = (bf16[512,128]{1,0:T(8,128)(2,1)S(1)}, bf16[512,128]{1,0:T(8,128)(2,1)}, u32[]{:S(2)}) copy-start(bf16[512,128]{1,0:T(8,128)(2,1)} %uk_ref.1) | copy-start | bytes 393220
  6.5 13.2 %copy-start.3 = (bf16[2048,128]{1,0:T(8,128)(2,1)S(1)}, bf16[2048,128]{1,0:T(8,128)(2,1)}, u32[]{:S(2)}) copy-start(bf16[2048,128]{1,0:T(8,128)(2,1)} %nope_ref.1) | copy-start | bytes 1572868
  6.6 100.8 %all-gather.2.cloned.1.call-start = ((), (), s32[]{:S(2)}) async-start(), calls=%async_computation.6 | async-start | bytes 4456448 | tf_op jit(solution)/shard_map/all_gather | solution.py:388
  9.4 1.0 copy-start.2
  10.4 0.7 copy-start.7
  12.5 16.1 %all-to-all-start = ((bf16[8,64,576]{2,1,0:T(8,128)(2,1)}), bf16[8,64,576]{2,1,0:T(8,128)(2,1)S(1)}, u32[]{:S(2)}, u32[]{:S(2)}) async-start(bf16[8,64,576]{2,1,0:T(8,128)(2,1)} %bitcast.4), calls=%async_computation | async-start | bytes 1310720 | tf_op jit(solution)/shard_map/all_to_all | solution.py:416
  28.7 9.8 %copy-start.25 = (bf16[512]{0:T(512)(128)(2,1)S(1)}, bf16[512]{0:T(512)(128)(2,1)}, u32[]{:S(2)}) copy-start(bf16[512]{0:T(512)(128)(2,1)} %param.28) | copy-start | bytes 3076
  30.3 36.8 %all-to-all-start.1 = ((bf16[16,72,576]{2,1,0:T(8,128)(2,1)}), bf16[16,72,576]{2,1,0:T(8,128)(2,1)S(1)}, u32[]{:S(2)}, u32[]{:S(2)}) async-start(bf16[16,72,576]{2,1,0:T(8,128)(2,1)} %maximum_maximum_fusion), calls=%async_computation.1 | async-start | bytes 2949120 | tf_op jit(solution)/shard_map/all_to_all | solution.py:462
  38.4 3.8 %copy-start.12 = (bf16[2048,64]{0,1:T(8,128)(2,1)S(1)}, bf16[2048,64]{0,1:T(8,128)(2,1)}, u32[]{:S(2)}) copy-start(bf16[2048,64]{0,1:T(8,128)(2,1)} %param.27) | copy-start | bytes 786436
  38.6 3.6 %copy-start.10 = (bf16[2048,512]{1,0:T(8,128)(2,1)S(1)}, bf16[2048,512]{1,0:T(8,128)(2,1)}, u32[]{:S(2)}) copy-start(bf16[2048,512]{1,0:T(8,128)(2,1)} %latent_ref.3) | copy-start | bytes 6291460
  42.2 2.5 copy-start.6
  44.7 32.6 %copy-start.5 = (bf16[512,128]{1,0:T(8,128)(2,1)S(1)}, bf16[512,128]{1,0:T(8,128)(2,1)}, u32[]{:S(2)}) copy-start(bf16[512,128]{1,0:T(8,128)(2,1)} %uv_ref.1) | copy-start | bytes 393220
  52.2 1.1 copy-start.13
  53.3 1.1 copy-start.8
  68.4 18.9 %all-to-all-start.2 = ((bf16[16,4,128]{2,1,0:T(4,128)(2,1)}), bf16[16,4,128]{2,1,0:T(4,128)(2,1)S(1)}, u32[]{:S(2)}, u32[]{:S(2)}) async-start(bf16[16,4,128]{2,1,0:T(4,128)(2,1)} %shard_map.211), calls=%async_computation.2 | async-start | bytes 32768 | tf_op jit(solution)/shard_map/all_to_all | solution.py:469
  77.2 1.3 copy-start.9
  78.6 1.3 copy-start.14
  87.3 8.6 %copy-start.21 = (s32[65,6]{0,1:T(8,128)S(1)}, s32[65,6]{0,1:T(8,128)}, u32[]{:S(2)}) copy-start(s32[65,6]{0,1:T(8,128)} %param.37) | copy-start | bytes 4684
  88.5 18.5 %all-to-all-start.3 = ((bf16[32,65,128]{2,1,0:T(8,128)(2,1)}), bf16[32,65,128]{2,1,0:T(8,128)(2,1)S(1)}, u32[]{:S(2)}, u32[]{:S(2)}) async-start(bf16[32,65,128]{2,1,0:T(8,128)(2,1)} %bitcast.12), calls=%async_computation.3 | async-start | bytes 1179648 | tf_op jit(solution)/shard_map/all_to_all | solution.py:479
  107.3 3.4 %copy-start.24 = (bf16[2048]{0:T(1024)(128)(2,1)S(1)}, bf16[2048]{0:T(1024)(128)(2,1)}, u32[]{:S(2)}) copy-start(bf16[2048]{0:T(1024)(128)(2,1)} %param.32) | copy-start | bytes 12292
  110.3 1.7 collective-permute-start
  113.5 0.7 copy-start.18
  118.5 8.8 %copy-start.15 = (bf16[1,2048,704]{1,2,0:T(8,128)(2,1)S(1)}, bf16[1,2048,704]{1,2,0:T(8,128)(2,1)}, u32[]{:S(2)}) copy-start(bf16[1,2048,704]{1,2,0:T(8,128)(2,1)} %param.35) | copy-start | bytes 8650756
  118.5 73.0 %all-to-all-start.4 = ((bf16[128,160,128]{2,1,0:T(8,128)(2,1)}), bf16[128,160,128]{2,1,0:T(8,128)(2,1)}, u32[]{:S(2)}, u32[]{:S(2)}) async-start(bf16[128,160,128]{2,1,0:T(8,128)(2,1)} %bitcast.62), calls=%async_computation.4 | async-start | bytes 10485760 | tf_op jit(solution)/shard_map/all_to_all | solution.py:509
  127.4 2.9 copy-start.16
  130.2 2.9 copy-start.17
  211.1 5.2 %copy-start.19 = (bf16[65,2048]{1,0:T(8,128)(2,1)S(1)}, bf16[65,2048]{1,0:T(8,128)(2,1)}, u32[]{:S(2)}) copy-start(bf16[65,2048]{1,0:T(8,128)(2,1)} %copy-done.18) | copy-start | bytes 798724
  211.1 5.2 %copy-start.20 = (bf16[2048,64]{0,1:T(8,128)(2,1)S(1)}, bf16[2048,64]{0,1:T(8,128)(2,1)}, u32[]{:S(2)}) copy-start(bf16[2048,64]{0,1:T(8,128)(2,1)} %param.33) | copy-start | bytes 786436
  211.1 70.9 %all-to-all-start.5 = ((bf16[128,160,128]{2,1,0:T(8,128)(2,1)}), bf16[128,160,128]{2,1,0:T(8,128)(2,1)}, u32[]{:S(2)}, u32[]{:S(2)}) async-start(bf16[128,160,128]{2,1,0:T(8,128)(2,1)} %bitcast.63), calls=%async_computation.5 | async-start | bytes 10485760 | tf_op jit(solution)/shard_map/all_to_all | solution.py:509
  282.0 4.3 %copy-start.1 = (bf16[128,2048]{1,0:T(8,128)(2,1)S(1)}, bf16[128,2048]{1,0:T(8,128)(2,1)}, u32[]{:S(2)}) copy-start(bf16[128,2048]{1,0:T(8,128)(2,1)} %param.31) | copy-start | bytes 1572868
Sparse Core Ops, SparseCore 0:
  9.5 64.9 all-gather.1

commit v5 on v4

--- a/solution.py
+++ b/solution.py
@@ -278,28 +278,32 @@
 
 def attend_kernel(scale, query_ref, message_ref, new_ref, seen_ref, uv_ref, out_ref):
     step = query_ref.shape[0]
-    first = pl.program_id(0) * step
-    query = query_ref[...]
-    old = message_ref[...].reshape(-1, KEY)
-    new = new_ref[...]
-    old_scores = dot_t(query, old) * scale + seen_ref[...]
-    new_scores = dot_t(query, new) * scale
-    rows = lax.broadcasted_iota(jnp.int32, new_scores.shape, 0) + first
-    keys = lax.broadcasted_iota(jnp.int32, new_scores.shape, 1)
-    new_scores = jnp.where(keys <= rows, new_scores, -jnp.inf)
-    top = jnp.maximum(
-        jnp.max(old_scores, axis=1, keepdims=True), jnp.max(new_scores, axis=1, keepdims=True)
-    )
-    old_raised = jnp.exp(old_scores - top)
-    new_raised = jnp.exp(new_scores - top)
-    total = jnp.sum(old_raised, axis=1, keepdims=True) + jnp.sum(
-        new_raised, axis=1, keepdims=True
-    )
-    share = 1.0 / total
-    attended = dot((old_raised * share).astype(BF16), old[:, :RANK]) + dot(
-        (new_raised * share).astype(BF16), new[:, :RANK]
-    )
-    out_ref[...] = dot(attended.astype(BF16), uv_ref[...]).astype(BF16)
+
+    def block(index):
+        query = query_ref[...]
+        old = message_ref[...].reshape(-1, KEY)
+        new = new_ref[: (index + 1) * step]
+        old_scores = dot_t(query, old) * scale + seen_ref[...]
+        new_scores = dot_t(query, new) * scale
+        rows = lax.broadcasted_iota(jnp.int32, new_scores.shape, 0) + index * step
+        keys = lax.broadcasted_iota(jnp.int32, new_scores.shape, 1)
+        new_scores = jnp.where(keys <= rows, new_scores, -jnp.inf)
+        top = jnp.maximum(
+            jnp.max(old_scores, axis=1, keepdims=True), jnp.max(new_scores, axis=1, keepdims=True)
+        )
+        old_raised = jnp.exp(old_scores - top)
+        new_raised = jnp.exp(new_scores - top)
+        total = jnp.sum(old_raised, axis=1, keepdims=True) + jnp.sum(
+            new_raised, axis=1, keepdims=True
+        )
+        share = 1.0 / total
+        attended = dot((old_raised * share).astype(BF16), old[:, :RANK]) + dot(
+            (new_raised * share).astype(BF16), new[:, :RANK]
+        )
+        out_ref[...] = dot(attended.astype(BF16), uv_ref[...]).astype(BF16)
+
+    for index in range(SPAN // step):
+        pl.when(pl.program_id(0) == index)(functools.partial(block, index))
 
 
 def attend(query, message, new, seen, uv, scale):
@@ -444,7 +448,7 @@
         axis=1,
     )
     positions = jnp.concatenate([span_len + jnp.arange(SPAN, dtype=jnp.int32), cache_len])
-    angles = rope_angles(positions, DR) + after(message)
+    angles = rope_angles(positions, DR) + after(message) + after(table)
     cosine, sine = jnp.cos(angles), jnp.sin(angles)
     query, new_keys = project(
         tokens,

time: 294 us -> 292 us (level)
    unnamed x58 -> x52, local copies, waits for them, and re-layouts: 14.1 us -> 12 us
  transfers between devices with their start and end apart: 8 -> 8, of which waited for: 6 -> 6; matrix products, arithmetic and copies ran while one was open for 8% -> 9% of each run, Pallas kernels for 6% -> 6%
where the time goes in v5:
time: 292 us; the launch traced here: 291 us
  waiting for transfers between devices  149 us (51%)
  Pallas kernels  43.1 us (15%)
  starting transfers between devices  40.3 us (14%)
  local copies, waits for them, and re-layouts  20.2 us (7%)
  other arithmetic  16.6 us (6%)
  between operations  16.5 us (6%)
  matrix products  5.66 us (2%)
    all_to_all x2, waiting for transfers between devices, spread(): lax.all_to_all(rows.reshape(device_count, capacity * blocks, LANES), FLAT...  122 us
    pallas_call x1, Pallas kernels, expert_rows(): pl.pallas_call(expert_kernel, grid=(rows // step,), in_specs=[pl.BlockSpe...  19.5 us
    unnamed x52, local copies, waits for them, and re-layouts  12 us
    all_to_all x1, waiting for transfers between devices, shards(): lax.all_to_all(message, 'exp', split_axis=0, concat_axis=0, tiled=True)  11.9 us
    all_to_all x2, starting transfers between devices, spread(): lax.all_to_all(rows.reshape(device_count, capacity * blocks, LANES), FLAT...  11.5 us
    all_to_all x1, waiting for transfers between devices, shards(): lax.all_to_all(jnp.broadcast_to(head_out.reshape(1, exp_count, rows_devic...  11.1 us
    all_to_all x1, starting transfers between devices, shards(): lax.all_to_all(own_out, 'exp', split_axis=0, concat_axis=0, tiled=True)  8.87 us
    all_to_all x1, starting transfers between devices, shards(): lax.all_to_all(message, 'exp', split_axis=0, concat_axis=0, tiled=True)  8.06 us
  transfers between devices with their start and end apart: 8, of which 6 were waited for; matrix products, arithmetic and copies ran while one was open for 9% of the time, Pallas kernels for 6%

profile of v5, /device:TPU:32, one launch (start us, length us, event | category | flops | bytes accessed | tf_op | source)
XLA Modules:
  0.0 291.3 jit_solution(3889701350400534264)
XLA Ops:
  6.6 1.0 copy-done
  7.6 0.7 constant_dynamic-slice_fusion.3
  8.3 1.0 reshape.215.rope_ref
  9.4 1.0 copy-done.2
  10.4 0.7 copy-done.7
  11.1 1.5 shard_map.208
  12.5 4.3 %all-to-all-start = ((bf16[8,64,576]{2,1,0:T(8,128)(2,1)}), bf16[8,64,576]{2,1,0:T(8,128)(2,1)S(1)}, u32[]{:S(2)}, u32[]{:S(2)}) async-start(bf16[8,64,576]{2,1,0:T(8,128)(2,1)} %bitcast.4), calls=%async_computation | async-start | bytes 1310720 | tf_op jit(solution)/shard_map/all_to_all | solution.py:420
  17.5 1.0 fusion.12
  18.5 1.1 fusion.27
  19.6 0.1 fusion.22
  19.8 1.2 convolution_convert_fusion.1
  21.3 0.3 select_reduce_fusion
  21.7 0.7 fusion.34
  22.4 0.8 fusion.31
  23.3 0.7 fusion.25
  24.0 0.6 iota_add_fusion
  24.6 0.7 fusion.26
  25.3 3.3 %all-to-all-done = bf16[8,64,576]{2,1,0:T(8,128)(2,1)S(1)} async-done(((bf16[8,64,576]{2,1,0:T(8,128)(2,1)}), bf16[8,64,576]{2,1,0:T(8,128)(2,1)S(1)}, u32[]{:S(2)}, u32[]{:S(2)}) %all-to-all-start) | async-done | bytes 589856 | tf_op jit(solution)/shard_map/all_to_all | solution.py:420
  28.7 1.6 maximum_maximum_fusion
  30.3 8.1 %all-to-all-start.1 = ((bf16[16,72,576]{2,1,0:T(8,128)(2,1)}), bf16[16,72,576]{2,1,0:T(8,128)(2,1)S(1)}, u32[]{:S(2)}, u32[]{:S(2)}) async-start(bf16[16,72,576]{2,1,0:T(8,128)(2,1)} %maximum_maximum_fusion), calls=%async_computation.1 | async-start | bytes 2949120 | tf_op jit(solution)/shard_map/all_to_all | solution.py:466
  38.6 0.5 slice.38
  39.7 0.5 slice.37
  40.9 2.0 fusion.11
  42.9 0.3 pad_maximum_fusion
  43.3 2.2 copy-done.6
  45.5 7.5 %shard_map.209 = (bf16[1040,576]{1,0:T(8,128)(2,1)S(1)}, bf16[1040,576]{1,0:T(8,128)(2,1)S(1)}) custom-call(bf16[1040,2048]{1,0:T(8,128)(2,1)S(1)} %copy-done.6, bf16[1,2048]{1,0:T(2,128)(2,1)S(1)} %broadcast_in_dim.122.gain_ref, bf16[2048,128]{1,0:T(8,128)(2,1)S(1)} %copy-done.3, bf16[64,2048]{1,0:T(8,128)(2,1)S(1)} %bitcast.61, ...), custom_call_target="tpu_custom_call" | custom-call | flops 3271557120 | bytes 9801728 | tf_op jit(solution)/shard_map/pallas_call | solution.py:229
  53.0 1.1 copy-done.13
  54.1 1.1 copy-done.8
  55.2 11.9 %all-to-all-done.1.message_ref = bf16[16,72,576]{2,1,0:T(8,128)(2,1)S(1)} async-done(((bf16[16,72,576]{2,1,0:T(8,128)(2,1)}), bf16[16,72,576]{2,1,0:T(8,128)(2,1)S(1)}, u32[]{:S(2)}, u32[]{:S(2)}) %all-to-all-start.1) | async-done | bytes 1327136 | tf_op jit(solution)/shard_map/all_to_all | solution.py:466
  67.1 1.2 shard_map.211
  68.3 8.9 %all-to-all-start.2 = ((bf16[16,4,128]{2,1,0:T(4,128)(2,1)}), bf16[16,4,128]{2,1,0:T(4,128)(2,1)S(1)}, u32[]{:S(2)}, u32[]{:S(2)}) async-start(bf16[16,4,128]{2,1,0:T(4,128)(2,1)} %shard_map.211), calls=%async_computation.2 | async-start | bytes 32768 | tf_op jit(solution)/shard_map/all_to_all | solution.py:473
  77.2 1.3 copy-done.9
  78.6 1.3 copy-done.14
  79.9 6.4 %shard_map.210 = bf16[1024,128]{1,0:T(8,128)(2,1)S(1)} custom-call(bf16[1040,576]{1,0:T(8,128)(2,1)S(1)} %copy-done.14, bf16[16,72,576]{2,1,0:T(8,128)(2,1)S(1)} %all-to-all-done.1.message_ref, bf16[1040,576]{1,0:T(8,128)(2,1)S(1)} %copy-done.9, f32[1,512]{1,0:T(1,128)S(1)} %select_n.78.seen_ref, bf16[512,128]{1,0:T(8,128)(2,1)S(1)} %copy-done.5), custom_call_target="tpu_custom_call" | custom-call | flops 3623878656 | bytes 4194304 | tf_op jit(solution)/shard_map/pallas_call | solution.py:318
  86.2 0.1 convolution_convert_fusion.2
  86.5 0.9 broadcast_in_dim.136
  87.4 7.4 %all-to-all-start.3 = ((bf16[32,65,128]{2,1,0:T(8,128)(2,1)}), bf16[32,65,128]{2,1,0:T(8,128)(2,1)S(1)}, u32[]{:S(2)}, u32[]{:S(2)}) async-start(bf16[32,65,128]{2,1,0:T(8,128)(2,1)} %bitcast.13), calls=%async_computation.3 | async-start | bytes 1179648 | tf_op jit(solution)/shard_map/all_to_all | solution.py:483
  94.8 11.1 %all-to-all-done.3 = bf16[32,65,128]{2,1,0:T(8,128)(2,1)S(1)} async-done(((bf16[32,65,128]{2,1,0:T(8,128)(2,1)}), bf16[32,65,128]{2,1,0:T(8,128)(2,1)S(1)}, u32[]{:S(2)}, u32[]{:S(2)}) %all-to-all-start.3) | async-done | bytes 532512 | tf_op jit(solution)/shard_map/all_to_all | solution.py:483
  106.1 0.1 copy.61
  106.3 2.9 %fusion.35 = f32[130,1024]{1,0:T(8,128)S(1)} fusion(bf16[130,2048]{1,0:T(8,128)(2,1)S(1)} %bitcast.71, bf16[2048,1024]{1,0:T(8,128)(2,1)} %all-gather.2.cloned.1.call-done), kind=kOutput, calls=%fused_computation.86 | convolution fusion | flops 545259520 | bytes 5259264 | tf_op jit(solution)/shard_map/dot_general | solution.py:50
  109.2 0.1 collective-permute-start
  109.4 0.7 add.191.table
  110.1 0.8 collective-permute-done
  111.0 1.2 fusion.3
  112.2 0.1 fusion.5
  112.4 0.7 slice.44.rows_ref
  113.2 3.6 %shard_map.212 = bf16[64,2,10,16,128]{4,3,2,1,0:T(8,128)(2,1)} custom-call(s32[640]{0:T(1024)} %add.191.table, bf16[65,16,128]{2,1,0:T(8,128)(2,1)} %slice.44.rows_ref), custom_call_target="tpu_custom_call" | custom-call | tf_op jit(solution)/shard_map/pallas_call | solution.py:91
  116.8 6.6 %all-to-all-start.4 = ((bf16[128,160,128]{2,1,0:T(8,128)(2,1)}), bf16[128,160,128]{2,1,0:T(8,128)(2,1)}, u32[]{:S(2)}, u32[]{:S(2)}) async-start(bf16[128,160,128]{2,1,0:T(8,128)(2,1)} %bitcast.63), calls=%async_computation.4 | async-start | bytes 10485760 | tf_op jit(solution)/shard_map/all_to_all | solution.py:513
  123.4 0.5 slice.43
  124.6 3.7 %add_bitcast_fusion.up_ref = bf16[1,704,2048]{2,1,0:T(8,128)(2,1)} fusion(bf16[1,2048,704]{1,2,0:T(8,128)(2,1)} %param.35, bf16[]{:T(256)} %bitcast.19), kind=kLoop, calls=%fused_computation | loop fusion | flops 1441792 | bytes 5767170 | tf_op jit(solution)/shard_map/add | solution.py:532
  128.3 1.8 broadcast_add_fusion.down_ref
  130.0 1.1 copy-done.16
  131.1 1.9 add_bitcast_fusion.1.gate_ref
  133.0 56.9 %all-to-all-done.4 = bf16[128,160,128]{2,1,0:T(8,128)(2,1)} async-done(((bf16[128,160,128]{2,1,0:T(8,128)(2,1)}), bf16[128,160,128]{2,1,0:T(8,128)(2,1)}, u32[]{:S(2)}, u32[]{:S(2)}) %all-to-all-start.4) | async-done | bytes 5242912 | tf_op jit(solution)/shard_map/all_to_all | solution.py:513
  189.9 19.5 %shard_map.213 = bf16[1280,16,128]{2,1,0:T(8,128)(2,1)} custom-call(bf16[1280,16,128]{2,1,0:T(8,128)(2,1)} %bitcast.18.x_ref, bf16[1,704,2048]{2,1,0:T(8,128)(2,1)} %add_bitcast_fusion.1.gate_ref, bf16[1,704,2048]{2,1,0:T(8,128)(2,1)} %add_bitcast_fusion.up_ref, bf16[1,704,2048]{2,1,0:T(8,128)(2,1)} %broadcast_add_fusion.down_ref), custom_call_target="tpu_custom_call" | custom-call | flops 11072962560 | bytes 10485760 | tf_op jit(solution)/shard_map/pallas_call | solution.py:172
  209.4 4.9 %all-to-all-start.5 = ((bf16[128,160,128]{2,1,0:T(8,128)(2,1)}), bf16[128,160,128]{2,1,0:T(8,128)(2,1)}, u32[]{:S(2)}, u32[]{:S(2)}) async-start(bf16[128,160,128]{2,1,0:T(8,128)(2,1)} %bitcast.64), calls=%async_computation.5 | async-start | bytes 10485760 | tf_op jit(solution)/shard_map/all_to_all | solution.py:513
  214.4 0.1 copy.52
  214.5 0.1 reshape.214.slots
  214.6 0.2 fusion.2
  214.9 0.1 copy.58
  215.1 0.1 div.30.gates
  215.3 64.9 %all-to-all-done.5 = bf16[128,160,128]{2,1,0:T(8,128)(2,1)} async-done(((bf16[128,160,128]{2,1,0:T(8,128)(2,1)}), bf16[128,160,128]{2,1,0:T(8,128)(2,1)}, u32[]{:S(2)}, u32[]{:S(2)}) %all-to-all-start.5) | async-done | bytes 5242912 | tf_op jit(solution)/shard_map/all_to_all | solution.py:513
  280.2 3.4 %shard_map.214 = bf16[65,16,128]{2,1,0:T(8,128)(2,1)S(1)} custom-call(s32[390]{0:T(512)S(1)} %reshape.214.slots, f32[390]{0:T(512)S(1)} %div.30.gates, bf16[1280,16,128]{2,1,0:T(8,128)(2,1)} %bitcast.23.half_ref, bf16[65,16,128]{2,1,0:T(8,128)(2,1)S(1)} %slice.45.resid_ref), custom_call_target="tpu_custom_call" | custom-call | tf_op jit(solution)/shard_map/pallas_call | solution.py:122
  283.6 0.8 copy.64
  (81 shorter events, 1.6 us)
Async XLA Ops:
  6.5 1.0 copy-start
  6.5 11.0 %copy-start.20 = (s32[16]{0:T(128)S(1)}, s32[16]{0:T(128)}, u32[]{:S(2)}) copy-start(s32[16]{0:T(128)} %param.42) | copy-start | bytes 196
  6.5 11.0 %copy-start.19 = (bf16[2048]{0:T(1024)(128)(2,1)S(1)}, bf16[2048]{0:T(1024)(128)(2,1)}, u32[]{:S(2)}) copy-start(bf16[2048]{0:T(1024)(128)(2,1)} %param.23) | copy-start | bytes 12292
  6.5 12.0 %copy-start.11 = (bf16[2048,64]{0,1:T(8,128)(2,1)S(1)}, bf16[2048,64]{0,1:T(8,128)(2,1)}, u32[]{:S(2)}) copy-start(bf16[2048,64]{0,1:T(8,128)(2,1)} %param.25) | copy-start | bytes 786436
  6.5 13.2 %copy-start.4 = (bf16[512,128]{1,0:T(8,128)(2,1)S(1)}, bf16[512,128]{1,0:T(8,128)(2,1)}, u32[]{:S(2)}) copy-start(bf16[512,128]{1,0:T(8,128)(2,1)} %uk_ref.1) | copy-start | bytes 393220
  6.5 13.2 %copy-start.3 = (bf16[2048,128]{1,0:T(8,128)(2,1)S(1)}, bf16[2048,128]{1,0:T(8,128)(2,1)}, u32[]{:S(2)}) copy-start(bf16[2048,128]{1,0:T(8,128)(2,1)} %nope_ref.1) | copy-start | bytes 1572868
  6.6 14.6 %copy-start.18 = (s32[65,6]{0,1:T(8,128)S(1)}, s32[65,6]{0,1:T(8,128)}, u32[]{:S(2)}) copy-start(s32[65,6]{0,1:T(8,128)} %param.37) | copy-start | bytes 4684
  6.6 99.7 %all-gather.2.cloned.1.call-start = ((), (), s32[]{:S(2)}) async-start(), calls=%async_computation.6 | async-start | bytes 4456448 | tf_op jit(solution)/shard_map/all_gather | solution.py:392
  9.4 1.0 copy-start.2
  10.4 0.7 copy-start.7
  12.5 16.1 %all-to-all-start = ((bf16[8,64,576]{2,1,0:T(8,128)(2,1)}), bf16[8,64,576]{2,1,0:T(8,128)(2,1)S(1)}, u32[]{:S(2)}, u32[]{:S(2)}) async-start(bf16[8,64,576]{2,1,0:T(8,128)(2,1)} %bitcast.4), calls=%async_computation | async-start | bytes 1310720 | tf_op jit(solution)/shard_map/all_to_all | solution.py:420
  28.7 9.7 %copy-start.22 = (bf16[512]{0:T(512)(128)(2,1)S(1)}, bf16[512]{0:T(512)(128)(2,1)}, u32[]{:S(2)}) copy-start(bf16[512]{0:T(512)(128)(2,1)} %param.28) | copy-start | bytes 3076
  30.3 36.8 %all-to-all-start.1 = ((bf16[16,72,576]{2,1,0:T(8,128)(2,1)}), bf16[16,72,576]{2,1,0:T(8,128)(2,1)S(1)}, u32[]{:S(2)}, u32[]{:S(2)}) async-start(bf16[16,72,576]{2,1,0:T(8,128)(2,1)} %maximum_maximum_fusion), calls=%async_computation.1 | async-start | bytes 2949120 | tf_op jit(solution)/shard_map/all_to_all | solution.py:466
  38.4 4.9 %copy-start.12 = (bf16[2048,64]{0,1:T(8,128)(2,1)S(1)}, bf16[2048,64]{0,1:T(8,128)(2,1)}, u32[]{:S(2)}) copy-start(bf16[2048,64]{0,1:T(8,128)(2,1)} %param.27) | copy-start | bytes 786436
  39.6 3.6 %copy-start.10 = (bf16[2048,512]{1,0:T(8,128)(2,1)S(1)}, bf16[2048,512]{1,0:T(8,128)(2,1)}, u32[]{:S(2)}) copy-start(bf16[2048,512]{1,0:T(8,128)(2,1)} %latent_ref.3) | copy-start | bytes 6291460
  43.3 2.2 copy-start.6
  45.5 31.8 %copy-start.5 = (bf16[512,128]{1,0:T(8,128)(2,1)S(1)}, bf16[512,128]{1,0:T(8,128)(2,1)}, u32[]{:S(2)}) copy-start(bf16[512,128]{1,0:T(8,128)(2,1)} %uv_ref.1) | copy-start | bytes 393220
  53.0 1.1 copy-start.13
  54.1 1.1 copy-start.8
  68.3 17.9 %all-to-all-start.2 = ((bf16[16,4,128]{2,1,0:T(4,128)(2,1)}), bf16[16,4,128]{2,1,0:T(4,128)(2,1)S(1)}, u32[]{:S(2)}, u32[]{:S(2)}) async-start(bf16[16,4,128]{2,1,0:T(4,128)(2,1)} %shard_map.211), calls=%async_computation.2 | async-start | bytes 32768 | tf_op jit(solution)/shard_map/all_to_all | solution.py:473
  77.2 1.3 copy-start.9
  78.5 1.3 copy-start.14
  87.4 18.5 %all-to-all-start.3 = ((bf16[32,65,128]{2,1,0:T(8,128)(2,1)}), bf16[32,65,128]{2,1,0:T(8,128)(2,1)S(1)}, u32[]{:S(2)}, u32[]{:S(2)}) async-start(bf16[32,65,128]{2,1,0:T(8,128)(2,1)} %bitcast.13), calls=%async_computation.3 | async-start | bytes 1179648 | tf_op jit(solution)/shard_map/all_to_all | solution.py:483
  106.2 3.9 %copy-start.21 = (bf16[2048]{0:T(1024)(128)(2,1)S(1)}, bf16[2048]{0:T(1024)(128)(2,1)}, u32[]{:S(2)}) copy-start(bf16[2048]{0:T(1024)(128)(2,1)} %param.32) | copy-start | bytes 12292
  109.2 1.7 collective-permute-start
  116.8 73.1 %all-to-all-start.4 = ((bf16[128,160,128]{2,1,0:T(8,128)(2,1)}), bf16[128,160,128]{2,1,0:T(8,128)(2,1)}, u32[]{:S(2)}, u32[]{:S(2)}) async-start(bf16[128,160,128]{2,1,0:T(8,128)(2,1)} %bitcast.63), calls=%async_computation.4 | async-start | bytes 10485760 | tf_op jit(solution)/shard_map/all_to_all | solution.py:513
  124.5 3.7 %copy-start.15 = (bf16[1,704,2048]{2,1,0:T(8,128)(2,1)S(1)}, bf16[1,704,2048]{2,1,0:T(8,128)(2,1)}, u32[]{:S(2)}) copy-start(bf16[1,704,2048]{2,1,0:T(8,128)(2,1)} %param.36) | copy-start | bytes 8650756
  128.3 2.9 copy-start.16
  209.4 5.2 %copy-start.17 = (bf16[2048,64]{0,1:T(8,128)(2,1)S(1)}, bf16[2048,64]{0,1:T(8,128)(2,1)}, u32[]{:S(2)}) copy-start(bf16[2048,64]{0,1:T(8,128)(2,1)} %param.33) | copy-start | bytes 786436
  209.4 70.7 %all-to-all-start.5 = ((bf16[128,160,128]{2,1,0:T(8,128)(2,1)}), bf16[128,160,128]{2,1,0:T(8,128)(2,1)}, u32[]{:S(2)}, u32[]{:S(2)}) async-start(bf16[128,160,128]{2,1,0:T(8,128)(2,1)} %bitcast.64), calls=%async_computation.5 | async-start | bytes 10485760 | tf_op jit(solution)/shard_map/all_to_all | solution.py:513
  280.2 4.3 %copy-start.1 = (bf16[128,2048]{1,0:T(8,128)(2,1)S(1)}, bf16[128,2048]{1,0:T(8,128)(2,1)}, u32[]{:S(2)}) copy-start(bf16[128,2048]{1,0:T(8,128)(2,1)} %param.31) | copy-start | bytes 1572868
Sparse Core Ops, SparseCore 0:
  9.5 64.8 all-gather.1
